TPU v7x, 32 devices: a whole 2x2x4 slice. The times are simulated.
32 devices in a mesh: band: 8 (over z, x), rows: 4 (over y, core).
Axes of the slice: x: 2, y: 2, z: 4, core: 2. Of those that a mesh axis runs over, the one named last changes fastest.
Arguments:
- pixels: bfloat16 [2048, 256, 196], P('band', 'rows'), may hold values from -6 to 6
- band_counts: int32 [8, 12], P('band'), may hold values from 1 to 202, 256 in all within a row
- band_waves: int32 [8, 256], P('band'), may hold values from 0 to 31
- wavelengths: float32 [32], replicated, may hold values from 0.4 to 2.5
- bias_token: float32 [128], replicated, may hold values from -6 to 6
- wave_qkv: float32 [128, 384], replicated, may hold values from -1 to 1
- wave_proj: float32 [128, 128], replicated, may hold values from -0.5 to 0.5
- wave_gain: float32 [128], replicated, may hold values from 0.5 to 1.5
- wave_shift: float32 [128], replicated, may hold values from -3 to 3
- wave_up: float32 [128, 2048], replicated, may hold values from -0.5 to 0.5
- wave_down: float32 [2048, 128], replicated, may hold values from -0.125 to 0.125
- kernel_gain: float32 [128], replicated, may hold values from 0.5 to 1.5
- kernel_shift: float32 [128], replicated, may hold values from -3 to 3
- bias_head: float32 [128, 768], replicated, may hold values from -0.5 to 0.5
- kernel_weight: bfloat16 [256, 128, 768], P('rows'), may hold values from -0.0078125 to 0.0078125
- attention_gain: float32 [768], replicated, may hold values from 0.5 to 1.5
- attention_shift: float32 [768], replicated, may hold values from -3 to 3
- block_qkv: bfloat16 [768, 2304], replicated, may hold values from -0.21875 to 0.21875
- block_proj: bfloat16 [768, 768], replicated, may hold values from -0.625 to 0.625
- hidden_gain: float32 [768], replicated, may hold values from 0.5 to 1.5
- hidden_shift: float32 [768], replicated, may hold values from -3 to 3
- block_up: bfloat16 [768, 3072], replicated, may hold values from -0.21875 to 0.21875
- block_down: bfloat16 [3072, 768], replicated, may hold values from -0.109375 to 0.109375
- cotangent: bfloat16 [18816, 768], P(('band', 'rows')), may hold values from -6 to 6
Outputs:
- layer_output: bfloat16 [18816, 768], P(('band', 'rows'))
- pixel_grad: bfloat16 [2048, 256, 196], P('band', 'rows')
- kernel_weight_grad: float32 [256, 128, 768], P('rows', 'band')
- bias_token_grad: float32 [128], replicated
- wave_qkv_grad: float32 [128, 384], replicated
- wave_proj_grad: float32 [128, 128], replicated
- wave_gain_grad: float32 [128], replicated
- wave_shift_grad: float32 [128], replicated
- wave_up_grad: float32 [128, 2048], replicated
- wave_down_grad: float32 [2048, 128], replicated
- kernel_gain_grad: float32 [128], replicated
- kernel_shift_grad: float32 [128], replicated
- bias_head_grad: float32 [128, 768], replicated
- attention_gain_grad: float32 [768], replicated
- attention_shift_grad: float32 [768], replicated
- block_qkv_grad: float32 [768, 2304], P('band')
- block_proj_grad: float32 [768, 768], P('band')
- hidden_gain_grad: float32 [768], replicated
- hidden_shift_grad: float32 [768], replicated
- block_up_grad: float32 [768, 3072], P('band')
- block_down_grad: float32 [3072, 768], P('band')
Inputs may be any that keep to these rules, and one draw needn't show every extreme that they name: `band_counts`: each row holds the band counts of the 12 images of one group; they sum to 256, the largest is exactly 202, and the slots of a group belong to its images in order.
All inputs are finite; a program needn't handle non-finite values.
Results may differ from a plain program's by a relative error of at most 0.015.
Values may be sent and summed in bfloat16 or wider, within the bound.
No kernel may reach another device: no remote copies, remote signals or barrier semaphores. Data moves between devices by JAX's collectives and lax.ppermute only.
A program may use at most 320 MiB of HBM per device.

v0:
```python
import math

import jax
import jax.numpy as jnp
from jax import lax
from jax.sharding import PartitionSpec as P

HEADS = 12
WD = 128
WHEADS = 4


highest = lax.Precision.HIGHEST


def matmul_high(left, right):
    return jnp.dot(left, right, precision=highest, preferred_element_type=jnp.float32)


def layer_norm(values, norm_gain, norm_shift, epsilon):
    centered = values - jnp.mean(values, axis=-1, keepdims=True)
    variance = jnp.mean(centered * centered, axis=-1, keepdims=True)
    return centered * lax.rsqrt(variance + epsilon) * norm_gain + norm_shift


def block_norm(values, norm_gain, norm_shift):
    return layer_norm(values, norm_gain, norm_shift, 1e-06)


def exact_gelu(values):
    return jax.nn.gelu(values, approximate=False)


def wave_embed(wavelengths):
    halfwidth = WD // 2
    indices = jnp.arange(halfwidth, dtype=jnp.float32)
    frequency = 1.0 / 10000.0 ** (indices / halfwidth)
    angles = (wavelengths * 1000.0)[:, None] * frequency[None, :]
    return jnp.concatenate([jnp.sin(angles), jnp.cos(angles)], axis=1)


def hypernet(embedded, params):
    (
        bias_token,
        wave_qkv,
        wave_proj,
        wave_gain,
        wave_shift,
        wave_up,
        wave_down,
        kernel_gain,
        kernel_shift,
        bias_head,
    ) = params
    sequence = jnp.concatenate([embedded, bias_token[None, :]], axis=0)
    length = sequence.shape[0]
    head_width = WD // WHEADS
    projected = matmul_high(sequence, wave_qkv).reshape(length, 3, WHEADS, head_width)
    scores = jnp.einsum(
        "qhd,khd->hqk", projected[:, 0], projected[:, 1], precision=highest
    ) / math.sqrt(head_width)
    weights = jax.nn.softmax(scores, axis=-1)
    attended = jnp.einsum("hqk,khd->qhd", weights, projected[:, 2], precision=highest).reshape(
        length, WD
    )
    normed_first = layer_norm(
        sequence + matmul_high(attended, wave_proj), wave_gain, wave_shift, 1e-05
    )
    widened = jax.nn.gelu(matmul_high(normed_first, wave_up), approximate=False)
    second = layer_norm(
        normed_first + matmul_high(widened, wave_down), kernel_gain, kernel_shift, 1e-05
    )
    return (second[:-1] + embedded, matmul_high(second[-1:], bias_head)[0])


def body(
    pixels,
    band_counts,
    band_waves,
    wavelengths,
    bias_token,
    wave_qkv,
    wave_proj,
    wave_gain,
    wave_shift,
    wave_up,
    wave_down,
    kernel_gain,
    kernel_shift,
    bias_head,
    kernel_weight,
    attention_gain,
    attention_shift,
    block_qkv,
    block_proj,
    hidden_gain,
    hidden_shift,
    block_up,
    block_down,
    cotangent,
):
    embedded = wave_embed(wavelengths)
    hyper_params = (
        bias_token,
        wave_qkv,
        wave_proj,
        wave_gain,
        wave_shift,
        wave_up,
        wave_down,
        kernel_gain,
        kernel_shift,
        bias_head,
    )

    def hyper_apply(params):
        return hypernet(embedded, params)

    (kernel_in, conv_bias), hyper_back = jax.vjp(hyper_apply, hyper_params)
    kernel_low = kernel_in.astype(jnp.bfloat16)
    kernel_local = jnp.einsum(
        "wk,qkc->wqc", kernel_low, kernel_weight, preferred_element_type=jnp.float32
    ).astype(jnp.bfloat16)
    slot_total = pixels.shape[0]
    positions = pixels.shape[1]
    patches = pixels.shape[2]
    images = band_counts.shape[1]
    width = kernel_weight.shape[2]
    block_slots = min(32, slot_total)
    block_count = slot_total // block_slots
    bounds = jnp.cumsum(band_counts[0])
    slot_index = jnp.arange(slot_total, dtype=jnp.int32)
    owners = jnp.sum((bounds[None, :] <= slot_index[:, None]).astype(jnp.int32), axis=1)
    pixel_blocks = pixels.reshape(block_count, block_slots, positions, patches)
    owner_blocks = owners.reshape(block_count, block_slots)
    wave_blocks = band_waves[0].reshape(block_count, block_slots)

    def embed_block(running, inputs):
        pixel_block, owner_block, wave_block = inputs
        chosen = kernel_local[wave_block]
        per_slot = jnp.einsum(
            "sqp,sqc->spc", pixel_block, chosen, preferred_element_type=jnp.float32
        )
        return (running + jax.ops.segment_sum(per_slot, owner_block, num_segments=images), None)

    summed = lax.scan(
        embed_block,
        jnp.zeros((images, patches, width), jnp.float32),
        (pixel_blocks, owner_blocks, wave_blocks),
    )[0]
    embedded_rows = (
        lax.psum_scatter(
            summed.reshape(images * patches, width), "rows", scatter_dimension=0, tiled=True
        )
        + conv_bias
    )
    row_count = embedded_rows.shape[0]
    local_images = row_count // patches
    head_size = width // HEADS
    divisor = math.sqrt(head_size)
    normed_in, norm_in_back = jax.vjp(block_norm, embedded_rows, attention_gain, attention_shift)
    normed_low = normed_in.astype(jnp.bfloat16)
    projected = jnp.dot(normed_low, block_qkv, preferred_element_type=jnp.float32).astype(
        jnp.bfloat16
    )
    heads_view = projected.reshape(local_images, patches, 3, HEADS, head_size)
    queries = heads_view[:, :, 0]
    keys_all = heads_view[:, :, 1]
    values_all = heads_view[:, :, 2]
    scores = (
        jnp.einsum("iqhd,ikhd->ihqk", queries, keys_all, preferred_element_type=jnp.float32)
        / divisor
    )
    log_total = jax.nn.logsumexp(scores, axis=-1, keepdims=True)
    probs_low = jnp.exp(scores - log_total).astype(jnp.bfloat16)
    mixed_low = (
        jnp.einsum("ihqk,ikhd->iqhd", probs_low, values_all, preferred_element_type=jnp.float32)
        .reshape(row_count, width)
        .astype(jnp.bfloat16)
    )
    middle = embedded_rows + jnp.dot(mixed_low, block_proj, preferred_element_type=jnp.float32)
    normed_mid, norm_mid_back = jax.vjp(block_norm, middle, hidden_gain, hidden_shift)
    mid_low = normed_mid.astype(jnp.bfloat16)
    upward = jnp.dot(mid_low, block_up, preferred_element_type=jnp.float32)
    activated, gelu_back = jax.vjp(exact_gelu, upward)
    activated_low = activated.astype(jnp.bfloat16)
    result = middle + jnp.dot(activated_low, block_down, preferred_element_type=jnp.float32)
    layer_output = result.astype(jnp.bfloat16)
    down_grad = jnp.einsum(
        "rf,rd->fd", activated_low, cotangent, preferred_element_type=jnp.float32
    )
    grad_activated = jnp.einsum(
        "rd,fd->rf", cotangent, block_down, preferred_element_type=jnp.float32
    )
    grad_up = gelu_back(grad_activated)[0].astype(jnp.bfloat16)
    up_grad = jnp.einsum("rd,rf->df", mid_low, grad_up, preferred_element_type=jnp.float32)
    grad_normed_mid = jnp.einsum("rf,df->rd", grad_up, block_up, preferred_element_type=jnp.float32)
    grad_mid_norm, hidden_gain_part, hidden_shift_part = norm_mid_back(grad_normed_mid)
    grad_middle = cotangent.astype(jnp.float32) + grad_mid_norm
    grad_attended = grad_middle.astype(jnp.bfloat16)
    proj_grad = jnp.einsum(
        "re,rd->ed", mixed_low, grad_attended, preferred_element_type=jnp.float32
    )
    grad_mixed = jnp.einsum(
        "rd,ed->re", grad_attended, block_proj, preferred_element_type=jnp.float32
    ).astype(jnp.bfloat16)
    grad_mixed_heads = grad_mixed.reshape(local_images, patches, HEADS, head_size)
    again = (
        jnp.einsum("iqhd,ikhd->ihqk", queries, keys_all, preferred_element_type=jnp.float32)
        / divisor
    )
    probs_again = jnp.exp(again - log_total)
    grad_probs = jnp.einsum(
        "iqhd,ikhd->ihqk", grad_mixed_heads, values_all, preferred_element_type=jnp.float32
    )
    grad_values = jnp.einsum(
        "ihqk,iqhd->ikhd",
        probs_again.astype(jnp.bfloat16),
        grad_mixed_heads,
        preferred_element_type=jnp.float32,
    )
    grad_scores = (
        probs_again * (grad_probs - jnp.sum(grad_probs * probs_again, axis=-1, keepdims=True))
    ).astype(jnp.bfloat16)
    grad_queries = (
        jnp.einsum("ihqk,ikhd->iqhd", grad_scores, keys_all, preferred_element_type=jnp.float32)
        / divisor
    )
    grad_keys = (
        jnp.einsum("ihqk,iqhd->ikhd", grad_scores, queries, preferred_element_type=jnp.float32)
        / divisor
    )
    grad_projected = (
        jnp.stack([grad_queries, grad_keys, grad_values], axis=2)
        .reshape(row_count, 3 * width)
        .astype(jnp.bfloat16)
    )
    qkv_grad = jnp.einsum(
        "rd,re->de", normed_low, grad_projected, preferred_element_type=jnp.float32
    )
    grad_normed_in = jnp.einsum(
        "re,de->rd", grad_projected, block_qkv, preferred_element_type=jnp.float32
    )
    grad_in_norm, attention_gain_part, attention_shift_part = norm_in_back(grad_normed_in)
    grad_embedded = grad_middle + grad_in_norm
    bias_grad, attention_gain_grad, attention_shift_grad, hidden_gain_grad, hidden_shift_grad = (
        lax.psum(
            (
                jnp.sum(grad_embedded, axis=0),
                attention_gain_part,
                attention_shift_part,
                hidden_gain_part,
                hidden_shift_part,
            ),
            ("band", "rows"),
        )
    )
    partial_qkv, partial_proj, partial_up, partial_down = (
        lax.psum_scatter(qkv_grad, "band", scatter_dimension=0, tiled=True),
        lax.psum_scatter(proj_grad, "band", scatter_dimension=0, tiled=True),
        lax.psum_scatter(up_grad, "band", scatter_dimension=0, tiled=True),
        lax.psum_scatter(down_grad, "band", scatter_dimension=0, tiled=True),
    )
    block_qkv_grad, block_proj_grad, block_up_grad, block_down_grad = (
        lax.psum(partial_qkv.astype(jnp.bfloat16), "rows").astype(jnp.float32),
        lax.psum(partial_proj.astype(jnp.bfloat16), "rows").astype(jnp.float32),
        lax.psum(partial_up.astype(jnp.bfloat16), "rows").astype(jnp.float32),
        lax.psum(partial_down.astype(jnp.bfloat16), "rows").astype(jnp.float32),
    )
    gathered = lax.all_gather(
        grad_embedded.astype(jnp.bfloat16), "rows", axis=0, tiled=True
    ).reshape(images, patches, width)
    wave_total = kernel_local.shape[0]
    kernel_wide = kernel_low.astype(jnp.float32)
    weight_wide = kernel_weight.astype(jnp.float32)

    def back_block(running, inputs):
        pixel_block, owner_block, wave_block = inputs
        chosen = kernel_local[wave_block]
        slot_grads = gathered[owner_block]
        pixel_part = jnp.einsum(
            "sqc,spc->sqp", chosen, slot_grads, preferred_element_type=jnp.float32
        ).astype(jnp.bfloat16)
        kernel_part = jnp.einsum(
            "sqp,spc->sqc", pixel_block, slot_grads, preferred_element_type=jnp.float32
        )
        return (
            running + jax.ops.segment_sum(kernel_part, wave_block, num_segments=wave_total),
            pixel_part,
        )

    kernel_sum, pixel_parts = lax.scan(
        back_block,
        jnp.zeros((wave_total, positions, width), jnp.float32),
        (pixel_blocks, owner_blocks, wave_blocks),
    )
    owned = lax.psum_scatter(kernel_sum, "band", scatter_dimension=0, tiled=True)
    band_place = lax.axis_index("band")
    owned_count = owned.shape[0]
    kernel_owned = lax.dynamic_slice_in_dim(kernel_wide, band_place * owned_count, owned_count, 0)
    partial_kernel = jnp.einsum(
        "wk,wqc->qkc", kernel_owned, owned, precision=highest, preferred_element_type=jnp.float32
    )
    kernel_weight_grad = lax.psum_scatter(partial_kernel, "band", scatter_dimension=1, tiled=True)
    owned_input = lax.psum(
        jnp.einsum(
            "wqc,qkc->wk", owned, weight_wide, precision=highest, preferred_element_type=jnp.float32
        ),
        "rows",
    )
    grad_kernel_in = lax.all_gather(owned_input, "band", axis=0, tiled=True)
    pixel_grad = pixel_parts.reshape(slot_total, positions, patches)
    hyper_grads = hyper_back((grad_kernel_in, bias_grad))[0]
    return (
        layer_output,
        pixel_grad,
        kernel_weight_grad,
        hyper_grads[0],
        hyper_grads[1],
        hyper_grads[2],
        hyper_grads[3],
        hyper_grads[4],
        hyper_grads[5],
        hyper_grads[6],
        hyper_grads[7],
        hyper_grads[8],
        hyper_grads[9],
        attention_gain_grad,
        attention_shift_grad,
        block_qkv_grad,
        block_proj_grad,
        hidden_gain_grad,
        hidden_shift_grad,
        block_up_grad,
        block_down_grad,
    )


def solution(mesh):
    in_specs = (
        P("band", "rows", None),
        P("band", None),
        P("band", None),
        P(),
        P(),
        P(),
        P(),
        P(),
        P(),
        P(),
        P(),
        P(),
        P(),
        P(),
        P("rows", None, None),
        P(),
        P(),
        P(),
        P(),
        P(),
        P(),
        P(),
        P(),
        P(("band", "rows"), None),
    )
    out_specs = (
        P(("band", "rows"), None),
        P("band", "rows", None),
        P("rows", "band", None),
        P(),
        P(),
        P(),
        P(),
        P(),
        P(),
        P(),
        P(),
        P(),
        P(),
        P(),
        P(),
        P("band", None),
        P("band", None),
        P(),
        P(),
        P("band", None),
        P("band", None),
    )
    return jax.shard_map(body, mesh=mesh, in_specs=in_specs, out_specs=out_specs, check_vma=False)
```

profile of v0, /device:TPU:0, one launch (start us, length us, event | category | flops | bytes accessed | tf_op | source)
XLA Modules:
  0.0 1829.6 jit_solution(17318997955293945865)
XLA Ops:
  32.8 13.6 copy.128
  49.9 418.0 %while.22 = (s32[]{:T(128)}, f32[12,196,768]{2,1,0:T(8,128)}, s32[8,32]{1,0:T(8,128)S(1)}, bf16[8,32,64,196]{3,2,1,0:T(8,128)(2,1)}, s32[8,32]{1,0:T(8,128)S(1)}, /*index=5*/bf16[32,64,768]{2,1,0:T(8,128)(2,1)}, s32[]{:T(128)}) while((s32[]{:T(128)}, f32[12,196,768]{2,1,0:T(8,128)}, s32[8,32]{1,0:T(8,128)S(1)}, ...), condition=%wide.region_10.11_spmd, body=%wide.region_8.10_spmd.sunk | while | flops 621380736 | bytes 87561184 | solution.py:146
  54.3 11.6 fusion.180
  65.9 36.3 %scatter_fusion = f32[12,196,768]{2,1,0:T(8,128)} fusion(f32[12,196,768]{2,1,0:T(8,128)} %get-tuple-element.424, s32[32]{0:T(128)S(1)} %fusion.178, f32[32,196,768]{2,1,0:T(8,128)} %fusion.180), kind=kCustom, calls=%fused_computation.3.clone.1 | custom fusion | flops 4816896 | bytes 57802880 | tf_op jit(solution)/shard_map/while/body/eval_jaxpr/scatter-add | solution.py:144
  118.2 36.2 %scatter_fusion = f32[12,196,768]{2,1,0:T(8,128)} fusion(f32[12,196,768]{2,1,0:T(8,128)} %get-tuple-element.424, s32[32]{0:T(128)S(1)} %fusion.178, f32[32,196,768]{2,1,0:T(8,128)} %fusion.180), kind=kCustom, calls=%fused_computation.3.clone.1 | custom fusion | flops 4816896 | bytes 57802880 | tf_op jit(solution)/shard_map/while/body/eval_jaxpr/scatter-add | solution.py:144
  170.3 36.2 %scatter_fusion = f32[12,196,768]{2,1,0:T(8,128)} fusion(f32[12,196,768]{2,1,0:T(8,128)} %get-tuple-element.424, s32[32]{0:T(128)S(1)} %fusion.178, f32[32,196,768]{2,1,0:T(8,128)} %fusion.180), kind=kCustom, calls=%fused_computation.3.clone.1 | custom fusion | flops 4816896 | bytes 57802880 | tf_op jit(solution)/shard_map/while/body/eval_jaxpr/scatter-add | solution.py:144
  222.5 36.2 %scatter_fusion = f32[12,196,768]{2,1,0:T(8,128)} fusion(f32[12,196,768]{2,1,0:T(8,128)} %get-tuple-element.424, s32[32]{0:T(128)S(1)} %fusion.178, f32[32,196,768]{2,1,0:T(8,128)} %fusion.180), kind=kCustom, calls=%fused_computation.3.clone.1 | custom fusion | flops 4816896 | bytes 57802880 | tf_op jit(solution)/shard_map/while/body/eval_jaxpr/scatter-add | solution.py:144
  274.7 36.2 %scatter_fusion = f32[12,196,768]{2,1,0:T(8,128)} fusion(f32[12,196,768]{2,1,0:T(8,128)} %get-tuple-element.424, s32[32]{0:T(128)S(1)} %fusion.178, f32[32,196,768]{2,1,0:T(8,128)} %fusion.180), kind=kCustom, calls=%fused_computation.3.clone.1 | custom fusion | flops 4816896 | bytes 57802880 | tf_op jit(solution)/shard_map/while/body/eval_jaxpr/scatter-add | solution.py:144
  315.3 11.6 fusion.180
  326.9 36.2 %scatter_fusion = f32[12,196,768]{2,1,0:T(8,128)} fusion(f32[12,196,768]{2,1,0:T(8,128)} %get-tuple-element.424, s32[32]{0:T(128)S(1)} %fusion.178, f32[32,196,768]{2,1,0:T(8,128)} %fusion.180), kind=kCustom, calls=%fused_computation.3.clone.1 | custom fusion | flops 4816896 | bytes 57802880 | tf_op jit(solution)/shard_map/while/body/eval_jaxpr/scatter-add | solution.py:144
  379.1 36.7 %scatter_fusion = f32[12,196,768]{2,1,0:T(8,128)} fusion(f32[12,196,768]{2,1,0:T(8,128)} %get-tuple-element.424, s32[32]{0:T(128)S(1)} %fusion.178, f32[32,196,768]{2,1,0:T(8,128)} %fusion.180), kind=kCustom, calls=%fused_computation.3.clone.1 | custom fusion | flops 4816896 | bytes 57802880 | tf_op jit(solution)/shard_map/while/body/eval_jaxpr/scatter-add | solution.py:144
  431.7 36.1 %scatter_fusion = f32[12,196,768]{2,1,0:T(8,128)} fusion(f32[12,196,768]{2,1,0:T(8,128)} %get-tuple-element.424, s32[32]{0:T(128)S(1)} %fusion.178, f32[32,196,768]{2,1,0:T(8,128)} %fusion.180), kind=kCustom, calls=%fused_computation.3.clone.1 | custom fusion | flops 4816896 | bytes 57802880 | tf_op jit(solution)/shard_map/while/body/eval_jaxpr/scatter-add | solution.py:144
  475.5 68.5 %fusion = f32[592,768]{1,0:T(8,128)} fusion(f32[2352,768]{1,0:T(8,128)} %reshape.371), kind=kCustom, calls=%all-reduce-scatter | all-reduce-scatter fusion | flops 1818625 | bytes 9044480
  618.9 20.5 %add_convert_fusion = (bf16[588,3072]{1,0:T(8,128)(2,1)S(1)}, f32[588,3072]{1,0:T(8,128)}) fusion(f32[588,3072]{1,0:T(8,128)S(1)} %fusion.94, bf16[588,768]{1,0:T(8,128)(2,1)S(1)} %copy-done.23, bf16[3072,768]{1,0:T(8,128)(2,1)S(1)} %bitcast.239), kind=kOutput, calls=%fused_computation.40 | convolution fusion | flops 2904588288 | bytes 23685120 | tf_op jit(solution)/shard_map/rd,fd->rf/dot_general | solution.py:192
  744.8 340.1 %while.23 = (s32[]{:T(128)}, f32[32,64,768]{2,1,0:T(8,128)}, bf16[8,32,64,196]{3,2,1,0:T(8,128)(2,1)}, s32[8,32]{1,0:T(8,128)}, bf16[8,32,64,196]{3,2,1,0:T(8,12...) while((s32[]{:T(128)}, f32[32,64,768]{2,1,0:T(8,128)}, ...), condition=%wide.region_25.26_spmd, body=%wide.region_23.25_spmd.sunk | while | flops 1235101952 | bytes 113976848 | solution.py:292
  771.1 16.0 scatter_fusion.1
  813.3 16.4 scatter_fusion.1
  856.0 16.0 scatter_fusion.1
  898.5 16.1 scatter_fusion.1
  941.0 16.0 scatter_fusion.1
  983.3 16.0 scatter_fusion.1
  1026.1 16.0 scatter_fusion.1
  1068.8 16.0 scatter_fusion.1
  1090.8 151.7 %reduce-scatter.19.cloned.1.call-done = f32[384,768]{1,0:T(8,128)} async-done(((f32[3072,768]{1,0:T(8,128)}), f32[384,768]{1,0:T(8,128)}) %reduce-scatter.19.cloned.1.call-update) | async-done | bytes 1179664 | tf_op jit(solution)/shard_map/reduce_scatter | solution.py:262
  1244.8 119.0 %reduce-scatter.9.cloned.1.call-done = f32[4,64,768]{2,1,0:T(8,128)} async-done(((f32[32,64,768]{2,1,0:T(8,128)}), f32[4,64,768]{2,1,0:T(8,128)}) %reduce-scatter.9.cloned.1.call-update) | async-done | bytes 786448 | tf_op jit(solution)/shard_map/reduce_scatter | solution.py:297
  1363.7 24.1 %convolution_bitcast_fusion = f32[64,128,768]{1,2,0:T(8,128)} fusion(f32[4,64,768]{2,1,0:T(8,128)} %reduce-scatter.9.cloned.1.call-done, bf16[32,128]{1,0:T(8,128)(2,1)} %copy-done.57, s32[]{:T(128)S(6)} %select_n.45), kind=kOutput, calls=%fused_computation.34 | convolution fusion | flops 301989888 | bytes 25953284 | tf_op jit(solution)/shard_map/wk,wqc->qkc/dot_general | solution.py:301
  1387.8 25.1 %copy.149 = f32[64,128,768]{2,0,1:T(8,128)} copy(f32[64,128,768]{1,2,0:T(8,128)} %convolution_bitcast_fusion) | data formatting | bytes 50331648 | tf_op jit(solution)/shard_map/wk,wqc->qkc/transpose | solution.py:301
  1414.9 44.6 %all-reduce.7 = (f32[768]{0:T(1024)S(1)}, f32[768]{0:T(1024)}, f32[768]{0:T(1024)}, f32[768]{0:T(1024)}, f32[768]{0:T(1024)}) all-reduce(f32[768]{0:T(1024)S(1)} %copy-done.67, f32[768]{0:T(1024)S(1)} %copy-done.91, f32[768]{0:T(1024)S(1)} %copy-done.92, f32[768]{0:T(1024)S(1)} %copy-done.89, ...), channel_id=1, replica_groups=mesh['band'=8,'rows'=4] {'band','rows'}, use_global_device_ids=true, to_apply=%region_29.30 | all-reduce | flops 3840 | bytes 30720 | tf_op jit(solution)/shard_map/psum | solution.py:247
  1468.9 13.5 copy.156
  1482.5 13.0 convolution_bitcast_fusion.4
  1502.3 27.9 %all-gather.1 = f32[8,4,128]{2,1,0:T(4,128)S(1)} all-gather(f32[1,4,128]{2,1,0:T(4,128)S(1)} %bitcast.232), channel_id=1, replica_groups=mesh['band'=8,'rows'=4] {'band'}, dimensions={0}, use_global_device_ids=true | all-gather | bytes 18432 | tf_op jit(solution)/shard_map/all_gather | solution.py:311
  1560.1 256.1 %reduce-scatter.11.cloned.1.call-done = f32[64,16,768]{2,0,1:T(8,128)} async-done(((f32[64,128,768]{2,0,1:T(8,128)}), f32[64,16,768]{2,0,1:T(8,128)}) %reduce-scatter.11.cloned.1.call-update) | async-done | bytes 3145744 | tf_op jit(solution)/shard_map/reduce_scatter | solution.py:304
  (480 shorter events, 591.4 us)
Async XLA Ops:
  8.0 554.7 %copy-start = (bf16[768,2304]{1,0:T(8,128)(2,1)S(1)}, bf16[768,2304]{1,0:T(8,128)(2,1)}, u32[]{:S(2)}) copy-start(bf16[768,2304]{1,0:T(8,128)(2,1)} %param.45) | copy-start | bytes 10616836
  8.0 728.7 %all-gather.4.cloned.1.call-start = ((), (), s32[]{:S(2)}) async-start(), calls=%async_computation.12 | async-start | bytes 4546560 | tf_op jit(solution)/shard_map/all_gather | solution.py:270
  475.5 73.2 %copy-start.97 = (u32[32]{0:T(128)S(1)}, u32[32]{0:T(128)}, u32[]{:S(2)}) copy-start(u32[32]{0:T(128)} %constant.209) | copy-start | bytes 388
  545.4 4.5 collective-permute-start
  548.6 60.6 %copy-start.54 = (f32[768]{0:T(1024)}, f32[768]{0:T(1024)S(1)}, u32[]{:S(2)}) copy-start(f32[768]{0:T(1024)S(1)} %convolution_reduce_fusion) | copy-start | bytes 9220
  612.5 31.0 %copy-start.10 = (f32[588,768]{1,0:T(8,128)}, f32[588,768]{1,0:T(8,128)S(1)}, u32[]{:S(2)}) copy-start(f32[588,768]{1,0:T(8,128)S(1)} %get-tuple-element.318) | copy-start | bytes 5419012
  612.9 26.5 %slice-start.2 = ((s8[4718592]{0:T(1024)(128)(4,1)}), s8[4194304]{0:T(1024)(128)(4,1)S(1)}, s32[]{:S(2)}) async-start(s8[4718592]{0:T(1024)(128)(4,1)} %bitcast.236), calls=%async_computation.16 | async-start | bytes 8388608
  618.9 20.5 %copy-start.18 = (f32[588,3072]{1,0:T(8,128)}, f32[588,3072]{1,0:T(8,128)S(1)}, u32[]{:S(2)}) copy-start(f32[588,3072]{1,0:T(8,128)S(1)} %fusion.94) | copy-start | bytes 21676036
  698.2 386.7 %reduce-scatter.15.cloned.1.call-start = ((), (), s32[]{:S(2)}) async-start(), calls=%async_computation.9 | async-start | bytes 2654208 | tf_op jit(solution)/shard_map/reduce_scatter | solution.py:260
  702.4 384.1 %reduce-scatter.13.cloned.1.call-start = ((), (), s32[]{:S(2)}) async-start(), calls=%async_computation.8 | async-start | bytes 7962624 | tf_op jit(solution)/shard_map/reduce_scatter | solution.py:259
  709.9 378.7 %reduce-scatter.17.cloned.1.call-start = ((), (), s32[]{:S(2)}) async-start(), calls=%async_computation.10 | async-start | bytes 10616832 | tf_op jit(solution)/shard_map/reduce_scatter | solution.py:261
  720.3 522.2 %reduce-scatter.19.cloned.1.call-start = ((), (), s32[]{:S(2)}) async-start(), calls=%async_computation.11 | async-start | bytes 10616832 | tf_op jit(solution)/shard_map/reduce_scatter | solution.py:262
  735.9 627.9 %reduce-scatter.9.cloned.1.call-start = ((), (), s32[]{:S(2)}) async-start(), calls=%async_computation.6 | async-start | bytes 7077888 | tf_op jit(solution)/shard_map/reduce_scatter | solution.py:297
  1084.9 468.3 %all-reduce.11.cloned.1.call-start = ((), (), s32[]{:S(2)}) async-start(), calls=%async_computation.13 | async-start | bytes 3538944 | tf_op jit(solution)/shard_map/psum | solution.py:265
  1244.7 571.5 %reduce-scatter.11.cloned.1.call-start = ((), (), s32[]{:S(2)}) async-start(), calls=%async_computation.7 | async-start | bytes 28311552 | tf_op jit(solution)/shard_map/reduce_scatter | solution.py:304
  1412.9 46.6 %copy-start.30 = (f32[128,768]{1,0:T(8,128)S(1)}, f32[128,768]{1,0:T(8,128)}, u32[]{:S(2)}) copy-start(f32[128,768]{1,0:T(8,128)} %param.41) | copy-start | bytes 1179652
  1413.0 48.3 %copy-start.12 = (f32[588,768]{1,0:T(8,128)S(1)}, f32[588,768]{1,0:T(8,128)}, u32[]{:S(2)}) copy-start(f32[588,768]{1,0:T(8,128)} %copy-done.10) | copy-start | bytes 5419012
  1482.5 50.7 %copy-start.21 = (f32[2048,128]{1,0:T(8,128)S(1)}, f32[2048,128]{1,0:T(8,128)}, u32[]{:S(2)}) copy-start(f32[2048,128]{1,0:T(8,128)} %param.38) | copy-start | bytes 3145732
  1482.5 50.7 %copy-start.27 = (f32[33,2048]{1,0:T(8,128)S(1)}, f32[33,2048]{1,0:T(8,128)}, u32[]{:S(2)}) copy-start(f32[33,2048]{1,0:T(8,128)} %copy-done.26) | copy-start | bytes 811012
  1482.5 50.8 %copy-start.29 = (f32[33,2048]{1,0:T(8,128)S(1)}, f32[33,2048]{1,0:T(8,128)}, u32[]{:S(2)}) copy-start(f32[33,2048]{1,0:T(8,128)} %copy-done.28) | copy-start | bytes 811012
  1482.5 52.0 %copy-start.33 = (f32[128,2048]{1,0:T(8,128)S(1)}, f32[128,2048]{1,0:T(8,128)}, u32[]{:S(2)}) copy-start(f32[128,2048]{1,0:T(8,128)} %param.37) | copy-start | bytes 3145732
  1482.5 52.0 %copy-start.72 = (f32[33]{0:T(128)S(1)}, f32[33]{0:T(128)}, u32[]{:S(2)}) copy-start(f32[33]{0:T(128)} %copy-done.71) | copy-start | bytes 400
  1482.5 52.0 %copy-start.76 = (f32[128]{0:T(128)S(1)}, f32[128]{0:T(128)}, u32[]{:S(2)}) copy-start(f32[128]{0:T(128)} %param.35) | copy-start | bytes 1540
  1482.5 52.0 %copy-start.78 = (f32[33]{0:T(128)S(1)}, f32[33]{0:T(128)}, u32[]{:S(2)}) copy-start(f32[33]{0:T(128)} %copy-done.77) | copy-start | bytes 400
  1495.6 42.0 %copy-start.40 = (f32[33,128]{1,0:T(8,128)S(1)}, f32[33,128]{1,0:T(8,128)}, u32[]{:S(2)}) copy-start(f32[33,128]{1,0:T(8,128)} %copy-done.39) | copy-start | bytes 50692
  1495.6 42.8 %copy-start.37 = (f32[33,384]{0,1:T(8,128)S(1)}, f32[33,384]{0,1:T(8,128)}, u32[]{:S(2)}) copy-start(f32[33,384]{0,1:T(8,128)} %copy-done.36) | copy-start | bytes 152068
  1495.6 42.8 %copy-start.66 = (f32[4,33]{1,0:T(4,128)S(1)}, f32[4,33]{1,0:T(4,128)}, u32[]{:S(2)}) copy-start(f32[4,33]{1,0:T(4,128)} %copy-done.65) | copy-start | bytes 1588
  1495.6 47.5 %copy-start.35 = (f32[128,384]{1,0:T(8,128)S(1)}, f32[128,384]{1,0:T(8,128)}, u32[]{:S(2)}) copy-start(f32[128,384]{1,0:T(8,128)} %param.33) | copy-start | bytes 589828
  1495.6 50.2 %copy-start.44 = (f32[32,64]{1,0:T(8,128)S(1)}, f32[32,64]{1,0:T(8,128)}, u32[]{:S(2)}) copy-start(f32[32,64]{1,0:T(8,128)} %copy-done.43) | copy-start | bytes 24580
  1495.6 50.2 %copy-start.46 = (f32[32,64]{1,0:T(8,128)S(1)}, f32[32,64]{1,0:T(8,128)}, u32[]{:S(2)}) copy-start(f32[32,64]{1,0:T(8,128)} %copy-done.45) | copy-start | bytes 24580
  1502.3 35.6 %copy-start.50 = (f32[128,128]{1,0:T(8,128)S(1)}, f32[128,128]{1,0:T(8,128)}, u32[]{:S(2)}) copy-start(f32[128,128]{1,0:T(8,128)} %param.34) | copy-start | bytes 196612
  1559.0 262.6 %copy-start.1 = (bf16[768,2304]{1,0:T(8,128)(2,1)S(1)}, bf16[768,2304]{1,0:T(8,128)(2,1)}, u32[]{:S(2)}) copy-start(bf16[768,2304]{1,0:T(8,128)(2,1)} %param.45) | copy-start | bytes 10616836
  (91 other events, 424.0 us)
Sparse Core Ops, SparseCore 0:
  698.3 38.4 all-gather.3
  1244.8 45.6 all-reduce.10
Sparse Core Ops, SparseCore 1:
  702.5 76.1 reduce-scatter.14
  782.3 127.7 reduce-scatter.12
  913.9 162.3 reduce-scatter.16
  1080.3 162.2 reduce-scatter.18
  1247.1 116.6 reduce-scatter.8
  1413.1 403.1 reduce-scatter.10
where the time goes:
time: 1840 us; the launch traced here: 1830 us
  waiting for transfers between devices  528 us (29%)
  other arithmetic  471 us (26%)
  matrix products  381 us (21%)
  local copies, waits for them, and re-layouts  282 us (15%)
  blocking collectives  148 us (8%)
    scatter-add x8, other arithmetic, embed_block(): jax.ops.segment_sum(per_slot, owner_block, num_segments=images)  290 us
    reduce_scatter x1, waiting for transfers between devices, body(): lax.psum_scatter(partial_kernel, 'band', scatter_dimension=1, tiled=True)  256 us
    reduce_scatter x1, waiting for transfers between devices, body(): lax.psum_scatter(down_grad, 'band', scatter_dimension=0, tiled=True)  152 us
    scatter-add x8, other arithmetic, back_block(): jax.ops.segment_sum(kernel_part, wave_block, num_segments=wave_total)  128 us
    reduce_scatter x1, waiting for transfers between devices, body(): lax.psum_scatter(kernel_sum, 'band', scatter_dimension=0, tiled=True)  119 us
    dot_general x8, matrix products, embed_block(): jnp.einsum('sqp,sqc->spc', pixel_block, chosen, preferred_element_type=jn...  92.9 us
    dot_general x8, matrix products, back_block(): jnp.einsum('sqc,spc->sqp', chosen, slot_grads, preferred_element_type=jnp...  73.3 us
    unnamed x1, blocking collectives  68.5 us
  transfers between devices with their start and end apart: 9, of which 4 were waited for; matrix products, arithmetic and copies ran while one was open for 28% of the time, Pallas kernels for 0%

commit v1 on v0

--- a/solution.py
+++ b/solution.py
@@ -1,9 +1,337 @@
+import functools
 import math
 
 import jax
 import jax.numpy as jnp
 from jax import lax
+from jax.experimental import pallas as pl
+from jax.experimental.pallas import tpu as pltpu
 from jax.sharding import PartitionSpec as P
+
+VMEM_LIMIT = 60 * 1024 * 1024
+STEPS = 8
+QUAD = 4
+LANES = 128
+
+
+def pad_rows(rows):
+    return (rows + 15) // 16 * 16
+
+
+def fill_starts(counts_ref, starts_ref):
+    images = counts_ref.shape[0]
+    total, big, most, first = 0, 0, counts_ref[0], 0
+    for m in range(images):
+        starts_ref[m] = jnp.int32(total)
+        if m:
+            better = counts_ref[m] > most
+            big = jnp.where(better, m, big)
+            first = jnp.where(better, total, first)
+            most = jnp.where(better, counts_ref[m], most)
+        total = total + counts_ref[m]
+    starts_ref[images] = jnp.int32(total)
+    return big, first, first + most
+
+
+def strided(ref, first, count, stride):
+    parts = [ref[c, pl.ds(first, count, stride=stride), :] for c in range(ref.shape[0])]
+    return jnp.concatenate(parts, axis=1)
+
+
+def embed_kernel(
+    counts_ref, waves_ref, kin_ref, weight_ref, pix_ref, out_ref, sums_ref, table_ref,
+    starts_ref, rows_ref, total_ref, keep_ref, acc_ref,
+):
+    step = pl.program_id(0)
+    waves, positions, patches = sums_ref.shape
+    images = counts_ref.shape[0]
+    per_step = weight_ref.shape[0]
+    chunk = pix_ref.shape[0]
+    big, big_lo, big_hi = fill_starts(counts_ref, starts_ref)
+
+    @pl.when(step == 0)
+    def _():
+        total_ref[...] = jnp.zeros_like(total_ref)
+
+    for q in range(per_step):
+        row = pl.multiple_of((step * per_step + q) * waves, waves)
+        made = jnp.dot(kin_ref[...], weight_ref[q], preferred_element_type=jnp.float32)
+        for c in range(rows_ref.shape[0]):
+            rows_ref[c, pl.ds(row, waves), :] = made[:, c * LANES : (c + 1) * LANES]
+    lo = step * chunk
+    hi = lo + chunk
+    cut_lo = jnp.clip(big_lo, lo, hi)
+    cut_hi = jnp.clip(big_hi, lo, hi)
+
+    def keep(s, carry):
+        keep_ref[s] = pix_ref[s - lo]
+        return carry
+
+    def gather(s, carry):
+        w = waves_ref[s]
+        total_ref[w] = total_ref[w] + pix_ref[s - lo].astype(jnp.float32)
+        return carry
+
+    lax.fori_loop(lo, cut_lo, keep, 0)
+    lax.fori_loop(cut_lo, cut_hi, gather, 0)
+    lax.fori_loop(cut_hi, hi, keep, 0)
+
+    @pl.when(step == pl.num_programs(0) - 1)
+    def _():
+        def turn(w, carry):
+            table_ref[w] = strided(rows_ref, w, positions, waves).astype(jnp.bfloat16)
+            sums_ref[w] = total_ref[w].astype(jnp.bfloat16)
+            return carry
+
+        lax.fori_loop(0, waves, turn, 0)
+        over_rows = (((0,), (0,)), ((), ()))
+
+        def product(left, right):
+            return lax.dot_general(left, right, over_rows, preferred_element_type=jnp.float32)
+
+        acc_ref[...] = jnp.zeros_like(acc_ref)
+        group = 8
+
+        def big_part(j, carry):
+            first = pl.multiple_of(j * group, group)
+            left = sums_ref[pl.ds(first, group)].reshape(group * positions, patches)
+            right = table_ref[pl.ds(first, group)].reshape(group * positions, -1)
+            acc_ref[:patches] += product(left, right)
+            return carry
+
+        lax.fori_loop(0, waves // group, big_part, 0)
+        out_ref[big] = acc_ref[...].astype(jnp.bfloat16)
+
+        def image(m, carry):
+            first, last = starts_ref[m], starts_ref[m + 1]
+
+            @pl.when(m != big)
+            def _():
+                acc_ref[...] = jnp.zeros_like(acc_ref)
+
+                def part(j, carry):
+                    lefts, rights = [], []
+                    for k in range(QUAD):
+                        s = first + j * QUAD + k
+                        here = jnp.minimum(s, last - 1)
+                        factor = jnp.where(s < last, 1.0, 0.0).astype(jnp.bfloat16)
+                        lefts.append(keep_ref[here] * factor)
+                        rights.append(table_ref[waves_ref[here]])
+                    acc_ref[:patches] += product(
+                        jnp.concatenate(lefts, axis=0), jnp.concatenate(rights, axis=0)
+                    )
+                    return carry
+
+                lax.fori_loop(0, (last - first + QUAD - 1) // QUAD, part, 0)
+                out_ref[m] = acc_ref[...].astype(jnp.bfloat16)
+
+            return carry
+
+        lax.fori_loop(0, images, image, 0)
+
+
+def embed_call(counts, band_waves, kernel_low, kernel_weight, pixels):
+    slots, positions, patches = pixels.shape
+    waves = kernel_low.shape[0]
+    depth, width = kernel_weight.shape[1:]
+    images = counts.shape[0]
+    padded = pad_rows(patches)
+    smem = pl.BlockSpec(memory_space=pltpu.SMEM)
+    return pl.pallas_call(
+        embed_kernel,
+        grid=(STEPS,),
+        in_specs=[
+            smem,
+            smem,
+            pl.BlockSpec((waves, depth), lambda i: (0, 0)),
+            pl.BlockSpec((positions // STEPS, depth, width), lambda i: (i, 0, 0)),
+            pl.BlockSpec((slots // STEPS, positions, patches), lambda i: (i, 0, 0)),
+        ],
+        out_specs=[
+            pl.BlockSpec((images, padded, width), lambda i: (0, 0, 0)),
+            pl.BlockSpec((waves, positions, patches), lambda i: (0, 0, 0)),
+            pl.BlockSpec((waves, positions, width), lambda i: (0, 0, 0)),
+        ],
+        out_shape=[
+            jax.ShapeDtypeStruct((images, padded, width), jnp.bfloat16),
+            jax.ShapeDtypeStruct((waves, positions, patches), jnp.bfloat16),
+            jax.ShapeDtypeStruct((waves, positions, width), jnp.bfloat16),
+        ],
+        scratch_shapes=[
+            pltpu.SMEM((images + 1,), jnp.int32),
+            pltpu.VMEM((width // LANES, positions * waves, LANES), jnp.float32),
+            pltpu.VMEM((waves, positions, patches), jnp.float32),
+            pltpu.VMEM((slots, positions, patches), jnp.bfloat16),
+            pltpu.VMEM((padded, width), jnp.float32),
+        ],
+        compiler_params=pltpu.CompilerParams(vmem_limit_bytes=VMEM_LIMIT),
+        name="embed",
+    )(counts, band_waves, kernel_low, kernel_weight, pixels)
+
+
+def embed_back_kernel(
+    counts_ref, waves_ref, grad_ref, table_ref, sums_ref, pix_ref, weight_ref,
+    pix_grad_ref, kernel_grad_ref, in_grad_ref,
+    starts_ref, owner_ref, wide_ref, big_ref,
+):
+    step = pl.program_id(0)
+    waves, positions, patches = sums_ref.shape
+    images = counts_ref.shape[0]
+    width = table_ref.shape[2]
+    chunk = pix_ref.shape[0]
+    slot_steps = waves_ref.shape[0] // chunk
+    big, big_lo, big_hi = fill_starts(counts_ref, starts_ref)
+    over_width = (((1,), (1,)), ((), ()))
+
+    @pl.when(step == 0)
+    def _():
+        for m in range(images):
+            def own(s, carry, m=m):
+                owner_ref[s] = jnp.int32(m)
+                return carry
+
+            lax.fori_loop(starts_ref[m], starts_ref[m + 1], own, 0)
+        group = 8
+        slope = grad_ref[big]
+
+        def big_part(j, carry):
+            first = pl.multiple_of(j * group, group)
+            rows = pl.ds(pl.multiple_of(j * group * positions, group * positions), group * positions)
+            left = table_ref[pl.ds(first, group)].reshape(group * positions, width)
+            both = lax.dot_general(left, slope, over_width, preferred_element_type=jnp.float32)
+            big_ref[pl.ds(first, group)] = (
+                both[:, :patches].astype(jnp.bfloat16).reshape(group, positions, patches)
+            )
+            left = sums_ref[pl.ds(first, group)].reshape(group * positions, patches)
+            made = jnp.dot(left, slope[:patches], preferred_element_type=jnp.float32)
+            for c in range(wide_ref.shape[0]):
+                wide_ref[c, rows, :] = made[:, c * LANES : (c + 1) * LANES]
+            return carry
+
+        lax.fori_loop(0, waves // group, big_part, 0)
+
+    @pl.when(step < slot_steps)
+    def _():
+        lo = step * chunk
+        hi = lo + chunk
+        cut_lo = jnp.clip(big_lo, lo, hi)
+        cut_hi = jnp.clip(big_hi, lo, hi)
+
+        def copy(s, carry):
+            pix_grad_ref[s - lo] = big_ref[waves_ref[s]]
+            return carry
+
+        lax.fori_loop(cut_lo, cut_hi, copy, 0)
+
+        def small(end):
+            def part(s):
+                m = owner_ref[s]
+                slope = grad_ref[m]
+                last = jnp.minimum(jnp.minimum(starts_ref[m + 1], end), s + QUAD)
+                lefts, rights, index = [], [], []
+                for k in range(QUAD):
+                    here = jnp.minimum(s + k, last - 1)
+                    factor = jnp.where(s + k < last, 1.0, 0.0).astype(jnp.bfloat16)
+                    index.append(here)
+                    lefts.append(table_ref[waves_ref[here]])
+                    rights.append(pix_ref[here - lo] * factor)
+                both = lax.dot_general(
+                    jnp.concatenate(lefts, axis=0),
+                    slope,
+                    over_width,
+                    preferred_element_type=jnp.float32,
+                )[:, :patches].astype(jnp.bfloat16)
+                more = jnp.dot(
+                    jnp.concatenate(rights, axis=0),
+                    slope[:patches],
+                    preferred_element_type=jnp.float32,
+                )
+                for k in range(QUAD):
+                    part_rows = slice(k * positions, (k + 1) * positions)
+                    pix_grad_ref[index[k] - lo] = both[part_rows]
+                    row = pl.multiple_of(waves_ref[index[k]] * positions, positions)
+                    for c in range(wide_ref.shape[0]):
+                        wide_ref[c, pl.ds(row, positions), :] += more[
+                            part_rows, c * LANES : (c + 1) * LANES
+                        ]
+                return last
+
+            return part
+
+        lax.while_loop(lambda s: s < cut_lo, small(cut_lo), lo)
+        lax.while_loop(lambda s: s < hi, small(hi), cut_hi)
+
+    @pl.when(step == slot_steps)
+    def _():
+        in_grad_ref[...] = jnp.zeros_like(in_grad_ref)
+
+    @pl.when(step >= slot_steps)
+    def _():
+        per_step = weight_ref.shape[0]
+        found = jnp.zeros(in_grad_ref.shape, jnp.float32)
+        for q in range(per_step):
+            place = (step - slot_steps) * per_step + q
+            rows = strided(wide_ref, place, waves, positions)
+            high = rows.astype(jnp.bfloat16)
+            kernel_grad_ref[q] = high
+            rest = (rows - high.astype(jnp.float32)).astype(jnp.bfloat16)
+            both = lax.dot_general(
+                jnp.concatenate([high, rest], axis=0),
+                weight_ref[q],
+                over_width,
+                preferred_element_type=jnp.float32,
+            )
+            found = found + (both[:waves] + both[waves:])
+        in_grad_ref[...] += found
+
+
+def embed_back_call(counts, band_waves, grads, table, sums, pixels, kernel_weight):
+    slots, positions, patches = pixels.shape
+    waves = table.shape[0]
+    depth, width = kernel_weight.shape[1:]
+    images, padded = grads.shape[:2]
+    smem = pl.BlockSpec(memory_space=pltpu.SMEM)
+    slot_block = (slots // STEPS, positions, patches)
+    weight_block = (positions // STEPS, depth, width)
+
+    def early(i):
+        return (jnp.minimum(i, STEPS - 1), 0, 0)
+
+    def late(i):
+        return (jnp.maximum(i - STEPS, 0), 0, 0)
+
+    return pl.pallas_call(
+        embed_back_kernel,
+        grid=(2 * STEPS,),
+        in_specs=[
+            smem,
+            smem,
+            pl.BlockSpec((images, padded, width), lambda i: (0, 0, 0)),
+            pl.BlockSpec((waves, positions, width), lambda i: (0, 0, 0)),
+            pl.BlockSpec((waves, positions, patches), lambda i: (0, 0, 0)),
+            pl.BlockSpec(slot_block, early),
+            pl.BlockSpec(weight_block, late),
+        ],
+        out_specs=[
+            pl.BlockSpec(slot_block, early),
+            pl.BlockSpec((positions // STEPS, waves, width), late),
+            pl.BlockSpec((waves, depth), lambda i: (0, 0)),
+        ],
+        out_shape=[
+            jax.ShapeDtypeStruct((slots, positions, patches), jnp.bfloat16),
+            jax.ShapeDtypeStruct((positions, waves, width), jnp.bfloat16),
+            jax.ShapeDtypeStruct((waves, depth), jnp.float32),
+        ],
+        scratch_shapes=[
+            pltpu.SMEM((images + 1,), jnp.int32),
+            pltpu.SMEM((slots,), jnp.int32),
+            pltpu.VMEM((width // LANES, waves * positions, LANES), jnp.float32),
+            pltpu.VMEM((waves, positions, patches), jnp.bfloat16),
+        ],
+        compiler_params=pltpu.CompilerParams(vmem_limit_bytes=VMEM_LIMIT),
+        name="embed_back",
+    )(counts, band_waves, grads, table, sums, pixels, kernel_weight)
+
 
 HEADS = 12
 WD = 128
@@ -71,6 +399,136 @@
         normed_first + matmul_high(widened, wave_down), kernel_gain, kernel_shift, 1e-05
     )
     return (second[:-1] + embedded, matmul_high(second[-1:], bias_head)[0])
+
+
+def swap_core(array):
+    return lax.ppermute(array, "rows", [(0, 1), (1, 0), (2, 3), (3, 2)])
+
+
+def swap_chip(array):
+    return lax.ppermute(array, "rows", [(0, 2), (2, 0), (1, 3), (3, 1)])
+
+
+def add_wide(left, right):
+    return left.astype(jnp.float32) + right.astype(jnp.float32)
+
+
+def rows_reduce(partial_rows):
+    place = lax.axis_index("rows")
+    chip, core = place // 2, place % 2
+    images = partial_rows.shape[0] // 4
+
+    def block(which_chip, which_core):
+        return lax.dynamic_slice_in_dim(
+            partial_rows, (which_chip * 2 + which_core) * images, images, 0
+        )
+
+    far = add_wide(block(1 - chip, core), swap_core(block(1 - chip, 1 - core)))
+    near = add_wide(block(chip, core), swap_core(block(chip, 1 - core)))
+    return near + swap_chip(far.astype(jnp.bfloat16)).astype(jnp.float32)
+
+
+def rows_gather(own):
+    place = lax.axis_index("rows")
+    chip, core = place // 2, place % 2
+    near = swap_core(own)
+    across = swap_chip(own)
+    far = swap_core(across)
+
+    def by_core(mine, other):
+        return jnp.concatenate(
+            [jnp.where(core == 0, mine, other), jnp.where(core == 0, other, mine)], axis=0
+        )
+
+    here, there = by_core(own, near), by_core(across, far)
+    return jnp.concatenate(
+        [jnp.where(chip == 0, here, there), jnp.where(chip == 0, there, here)], axis=0
+    )
+
+
+def weight_reduce(grad):
+    core = lax.axis_index("rows") % 2
+    half = grad.shape[1] // 2
+    low = grad.astype(jnp.bfloat16)
+    kept = lax.dynamic_slice_in_dim(low, core * half, half, 1)
+    sent = lax.dynamic_slice_in_dim(low, (1 - core) * half, half, 1)
+    pair = add_wide(kept, swap_core(sent)).astype(jnp.bfloat16)
+    part = lax.psum_scatter(pair, "band", scatter_dimension=0, tiled=True)
+    whole = add_wide(part, swap_chip(part)).astype(jnp.bfloat16)
+    other = swap_core(whole)
+    return jnp.where(
+        core == 0,
+        jnp.concatenate([whole, other], axis=1),
+        jnp.concatenate([other, whole], axis=1),
+    ).astype(jnp.float32)
+
+
+def slot_masks(counts, slot_waves, waves):
+    index = jnp.arange(counts.shape[0])
+    ends = jnp.sum(jnp.where(index[None, :] <= index[:, None], counts[None, :], 0), axis=1)
+    slots = jnp.arange(slot_waves.shape[0])
+    owners = jnp.sum((ends[None, :] <= slots[:, None]).astype(jnp.int32), axis=1)
+    return (
+        (owners[:, None] == index[None, :]).astype(jnp.bfloat16),
+        (slot_waves[:, None] == jnp.arange(waves)[None, :]).astype(jnp.bfloat16),
+    )
+
+
+def embed_plain(counts, slot_waves, kernel_low, kernel_weight, pixels):
+    slots, positions, patches = pixels.shape
+    table = jnp.einsum(
+        "wk,qkc->wqc", kernel_low, kernel_weight, preferred_element_type=jnp.float32
+    ).astype(jnp.bfloat16)
+    of_image, of_wave = slot_masks(counts, slot_waves, table.shape[0])
+    chunk = min(16, slots)
+
+    def part(running, inputs):
+        pixel, image, wave = inputs
+        chosen = jnp.einsum("sw,wqc->sqc", wave, table)
+        rows = jnp.einsum("sqp,sqc->spc", pixel, chosen, preferred_element_type=jnp.float32)
+        image = image.astype(jnp.float32)
+        return (running + jnp.einsum("si,spc->ipc", image, rows, precision=highest), None)
+
+    shape = (counts.shape[0], patches, table.shape[2])
+    total = lax.scan(
+        part,
+        jnp.zeros(shape, jnp.float32),
+        tuple(a.reshape(-1, chunk, *a.shape[1:]) for a in (pixels, of_image, of_wave)),
+    )[0]
+    extra = pad_rows(patches) - patches
+    return (jnp.pad(total.astype(jnp.bfloat16), ((0, 0), (0, extra), (0, 0))), table)
+
+
+def embed_back_plain(counts, slot_waves, grads, table, pixels, kernel_weight):
+    slots, positions, patches = pixels.shape
+    waves, _, width = table.shape
+    of_image, of_wave = slot_masks(counts, slot_waves, waves)
+    grads = grads[:, :patches]
+    chunk = min(16, slots)
+
+    def part(running, inputs):
+        pixel, image, wave = inputs
+        chosen = jnp.einsum("sw,wqc->sqc", wave, table)
+        slope = jnp.einsum("si,ipc->spc", image, grads)
+        own = jnp.einsum("sqc,spc->sqp", chosen, slope, preferred_element_type=jnp.float32)
+        more = jnp.einsum("sqp,spc->sqc", pixel, slope, preferred_element_type=jnp.float32)
+        wave = wave.astype(jnp.float32)
+        added = jnp.einsum("sw,sqc->qwc", wave, more, precision=highest)
+        return (running + added, own.astype(jnp.bfloat16))
+
+    kernel_grad, pixel_grad = lax.scan(
+        part,
+        jnp.zeros((positions, waves, width), jnp.float32),
+        tuple(a.reshape(-1, chunk, *a.shape[1:]) for a in (pixels, of_image, of_wave)),
+    )
+    in_part = jnp.einsum(
+        "qwc,qkc->wk",
+        kernel_grad,
+        kernel_weight.astype(jnp.float32),
+        precision=highest,
+        preferred_element_type=jnp.float32,
+    )
+    return (pixel_grad.reshape(pixels.shape), kernel_grad.astype(jnp.bfloat16), in_part)
 
 
 def body(
@@ -118,41 +576,22 @@
 
     (kernel_in, conv_bias), hyper_back = jax.vjp(hyper_apply, hyper_params)
     kernel_low = kernel_in.astype(jnp.bfloat16)
-    kernel_local = jnp.einsum(
-        "wk,qkc->wqc", kernel_low, kernel_weight, preferred_element_type=jnp.float32
-    ).astype(jnp.bfloat16)
-    slot_total = pixels.shape[0]
-    positions = pixels.shape[1]
-    patches = pixels.shape[2]
-    images = band_counts.shape[1]
-    width = kernel_weight.shape[2]
-    block_slots = min(32, slot_total)
-    block_count = slot_total // block_slots
-    bounds = jnp.cumsum(band_counts[0])
-    slot_index = jnp.arange(slot_total, dtype=jnp.int32)
-    owners = jnp.sum((bounds[None, :] <= slot_index[:, None]).astype(jnp.int32), axis=1)
-    pixel_blocks = pixels.reshape(block_count, block_slots, positions, patches)
-    owner_blocks = owners.reshape(block_count, block_slots)
-    wave_blocks = band_waves[0].reshape(block_count, block_slots)
-
-    def embed_block(running, inputs):
-        pixel_block, owner_block, wave_block = inputs
-        chosen = kernel_local[wave_block]
-        per_slot = jnp.einsum(
-            "sqp,sqc->spc", pixel_block, chosen, preferred_element_type=jnp.float32
+    counts = band_counts[0]
+    slot_waves = band_waves[0]
+    slot_total, positions, patches = pixels.shape
+    images = counts.shape[0]
+    waves, width = kernel_low.shape[0], kernel_weight.shape[2]
+    fits = waves * positions * width <= 1 << 21
+    if fits:
+        partial_rows, wave_sums, kernel_table = embed_call(
+            counts, slot_waves, kernel_low, kernel_weight, pixels
         )
-        return (running + jax.ops.segment_sum(per_slot, owner_block, num_segments=images), None)
-
-    summed = lax.scan(
-        embed_block,
-        jnp.zeros((images, patches, width), jnp.float32),
-        (pixel_blocks, owner_blocks, wave_blocks),
-    )[0]
+    else:
+        partial_rows, kernel_table = embed_plain(
+            counts, slot_waves, kernel_low, kernel_weight, pixels
+        )
     embedded_rows = (
-        lax.psum_scatter(
-            summed.reshape(images * patches, width), "rows", scatter_dimension=0, tiled=True
-        )
-        + conv_bias
+        rows_reduce(partial_rows)[:, :patches].reshape(-1, width) + conv_bias
     )
     row_count = embedded_rows.shape[0]
     local_images = row_count // patches
@@ -243,73 +682,47 @@
     )
     grad_in_norm, attention_gain_part, attention_shift_part = norm_in_back(grad_normed_in)
     grad_embedded = grad_middle + grad_in_norm
+    grad_rows = jnp.pad(
+        grad_embedded.astype(jnp.bfloat16).reshape(local_images, patches, width),
+        ((0, 0), (0, pad_rows(patches) - patches), (0, 0)),
+    )
+    gathered = rows_gather(grad_rows)
+    block_down_grad = weight_reduce(down_grad)
+    block_up_grad = weight_reduce(up_grad)
+    block_proj_grad = weight_reduce(proj_grad)
+    block_qkv_grad = weight_reduce(qkv_grad)
+    if fits:
+        pixel_grad, kernel_grad, in_part = embed_back_call(
+            counts, slot_waves, gathered, kernel_table, wave_sums, pixels, kernel_weight
+        )
+    else:
+        pixel_grad, kernel_grad, in_part = embed_back_plain(
+            counts, slot_waves, gathered, kernel_table, pixels, kernel_weight
+        )
+    vectors = jnp.stack(
+        [
+            jnp.sum(grad_embedded, axis=0),
+            attention_gain_part,
+            attention_shift_part,
+            hidden_gain_part,
+            hidden_shift_part,
+        ]
+    )
+    summed = lax.psum(
+        jnp.concatenate([in_part, vectors.reshape(-1, in_part.shape[1])], axis=0),
+        ("band", "rows"),
+    )
+    grad_kernel_in = summed[:waves]
     bias_grad, attention_gain_grad, attention_shift_grad, hidden_gain_grad, hidden_shift_grad = (
-        lax.psum(
-            (
-                jnp.sum(grad_embedded, axis=0),
-                attention_gain_part,
-                attention_shift_part,
-                hidden_gain_part,
-                hidden_shift_part,
-            ),
-            ("band", "rows"),
-        )
-    )
-    partial_qkv, partial_proj, partial_up, partial_down = (
-        lax.psum_scatter(qkv_grad, "band", scatter_dimension=0, tiled=True),
-        lax.psum_scatter(proj_grad, "band", scatter_dimension=0, tiled=True),
-        lax.psum_scatter(up_grad, "band", scatter_dimension=0, tiled=True),
-        lax.psum_scatter(down_grad, "band", scatter_dimension=0, tiled=True),
-    )
-    block_qkv_grad, block_proj_grad, block_up_grad, block_down_grad = (
-        lax.psum(partial_qkv.astype(jnp.bfloat16), "rows").astype(jnp.float32),
-        lax.psum(partial_proj.astype(jnp.bfloat16), "rows").astype(jnp.float32),
-        lax.psum(partial_up.astype(jnp.bfloat16), "rows").astype(jnp.float32),
-        lax.psum(partial_down.astype(jnp.bfloat16), "rows").astype(jnp.float32),
-    )
-    gathered = lax.all_gather(
-        grad_embedded.astype(jnp.bfloat16), "rows", axis=0, tiled=True
-    ).reshape(images, patches, width)
-    wave_total = kernel_local.shape[0]
-    kernel_wide = kernel_low.astype(jnp.float32)
-    weight_wide = kernel_weight.astype(jnp.float32)
-
-    def back_block(running, inputs):
-        pixel_block, owner_block, wave_block = inputs
-        chosen = kernel_local[wave_block]
-        slot_grads = gathered[owner_block]
-        pixel_part = jnp.einsum(
-            "sqc,spc->sqp", chosen, slot_grads, preferred_element_type=jnp.float32
-        ).astype(jnp.bfloat16)
-        kernel_part = jnp.einsum(
-            "sqp,spc->sqc", pixel_block, slot_grads, preferred_element_type=jnp.float32
-        )
-        return (
-            running + jax.ops.segment_sum(kernel_part, wave_block, num_segments=wave_total),
-            pixel_part,
-        )
-
-    kernel_sum, pixel_parts = lax.scan(
-        back_block,
-        jnp.zeros((wave_total, positions, width), jnp.float32),
-        (pixel_blocks, owner_blocks, wave_blocks),
-    )
-    owned = lax.psum_scatter(kernel_sum, "band", scatter_dimension=0, tiled=True)
-    band_place = lax.axis_index("band")
-    owned_count = owned.shape[0]
-    kernel_owned = lax.dynamic_slice_in_dim(kernel_wide, band_place * owned_count, owned_count, 0)
-    partial_kernel = jnp.einsum(
-        "wk,wqc->qkc", kernel_owned, owned, precision=highest, preferred_element_type=jnp.float32
-    )
-    kernel_weight_grad = lax.psum_scatter(partial_kernel, "band", scatter_dimension=1, tiled=True)
-    owned_input = lax.psum(
-        jnp.einsum(
-            "wqc,qkc->wk", owned, weight_wide, precision=highest, preferred_element_type=jnp.float32
-        ),
-        "rows",
-    )
-    grad_kernel_in = lax.all_gather(owned_input, "band", axis=0, tiled=True)
-    pixel_grad = pixel_parts.reshape(slot_total, positions, patches)
+        summed[waves:].reshape(5, width)
+    )
+    owned = lax.psum_scatter(kernel_grad, "band", scatter_dimension=0, tiled=True)
+    owned_weight = jnp.einsum(
+        "wk,qwc->qkc", kernel_low, owned, preferred_element_type=jnp.float32
+    ).astype(jnp.bfloat16)
+    kernel_weight_grad = lax.all_to_all(
+        owned_weight, "band", split_axis=1, concat_axis=0, tiled=True
+    ).astype(jnp.float32)
     hyper_grads = hyper_back((grad_kernel_in, bias_grad))[0]
     return (
         layer_output,

time: 1840 us -> 678 us (0.37)
  other arithmetic: 471 us -> 72 us
  waiting for transfers between devices: 528 us -> 198 us
  matrix products: 381 us -> 126 us
  local copies, waits for them, and re-layouts: 282 us -> 136 us
  blocking collectives: 148 us -> 42.1 us
  Pallas kernels: 0 us -> 62.4 us
    scatter-add x16 -> x0, other arithmetic: 419 us -> none  [the longest x8 290 us: embed_block(): jax.ops.segment_sum(per_slot, owner_block, num_segments=images)]
    reduce_scatter x6 -> x5, waiting for transfers between devices: 527 us -> 147 us  [the longest x4 147 us: weight_reduce(): part = lax.psum_scatter(pair, 'band', scatter_dimension=0, tiled=True)]
    dot_general x27 -> x1, matrix products: 257 us -> 2.82 us  [body(): jnp.einsum('wk,qwc->qkc', kernel_low, owned, preferred_element_type=jnp.f...]
    gather x24 -> x0, local copies, waits for them, and re-layouts: 114 us -> none  [the longest x8 60.8 us: back_block(): slot_grads = gathered[owner_block]]
    unnamed x1 -> x0, blocking collectives: 68.5 us -> none
    pallas_call x0 -> x2, Pallas kernels: none -> 62.4 us  [the longest x1 33.7 us: embed_back_call(): pl.pallas_call(embed_back_kernel, grid=(2 * STEPS,), in_specs=[smem, smem...]
    ppermute x0 -> x18, waiting for transfers between devices: none -> 50.9 us  [the longest x6 42.1 us: swap_chip(): return lax.ppermute(array, 'rows', [(0, 2), (2, 0), (1, 3), (3, 1)])]
    all_gather x1 -> x0, blocking collectives: 27.9 us -> none  [body(): grad_kernel_in = lax.all_gather(owned_input, 'band', axis=0, tiled=True)]
  transfers between devices with their start and end apart: 9 -> 24, of which waited for: 4 -> 8; matrix products, arithmetic and copies ran while one was open for 28% -> 21% of each run, Pallas kernels for 0% -> 5%
where the time goes in v1:
time: 678 us; the launch traced here: 671 us
  waiting for transfers between devices  198 us (29%)
  local copies, waits for them, and re-layouts  136 us (20%)
  matrix products  126 us (19%)
  other arithmetic  72 us (11%)
  Pallas kernels  62.4 us (9%)
  blocking collectives  42.1 us (6%)
  starting transfers between devices  18.7 us (3%)
  between operations  15.4 us (2%)
    reduce_scatter x4, waiting for transfers between devices, weight_reduce(): part = lax.psum_scatter(pair, 'band', scatter_dimension=0, tiled=True)  147 us
    unnamed x175, local copies, waits for them, and re-layouts  55.3 us
    psum x1, blocking collectives, body(): lax.psum(jnp.concatenate([in_part, vectors.reshape(-1, in_part.shape[1])]...  42.1 us
    ppermute x6, waiting for transfers between devices, swap_chip(): return lax.ppermute(array, 'rows', [(0, 2), (2, 0), (1, 3), (3, 1)])  42.1 us
    pallas_call x1, Pallas kernels, embed_back_call(): pl.pallas_call(embed_back_kernel, grid=(2 * STEPS,), in_specs=[smem, smem...  33.7 us
    pallas_call x1, Pallas kernels, embed_call(): pl.pallas_call(embed_kernel, grid=(STEPS,), in_specs=[smem, smem, pl.Bloc...  28.6 us
    dot_general x13, matrix products, matmul_high(): jnp.dot(left, right, precision=highest, preferred_element_type=jnp.float32)  26.1 us
    dot_general x1, matrix products, body(): jnp.einsum('rd,fd->rf', cotangent, block_down, preferred_element_type=jnp...  20.7 us
  transfers between devices with their start and end apart: 24, of which 8 were waited for; matrix products, arithmetic and copies ran while one was open for 21% of the time, Pallas kernels for 5%

profile of v1, /device:TPU:0, one launch (start us, length us, event | category | flops | bytes accessed | tf_op | source)
XLA Modules:
  0.0 671.0 jit_solution(13246520171837157214)
XLA Ops:
  18.4 13.8 %copy.123.pix_ref = bf16[256,64,196]{2,1,0:T(8,128)(2,1)} copy(bf16[256,64,196]{0,1,2:T(8,128)(2,1)} %param.24) | data formatting | bytes 12845056 | tf_op args[0]
  32.3 28.6 %embed.1 = (bf16[12,208,768]{2,1,0:T(8,128)(2,1)}, bf16[32,64,196]{2,1,0:T(8,128)(2,1)}, bf16[32,64,768]{2,1,0:T(8,128)(2,1)}) custom-call(s32[12]{0:T(128)} %bitcast.172, s32[256]{0:T(256)} %bitcast.170, bf16[32,128]{1,0:T(8,128)(2,1)} %fusion.48.kin_ref, bf16[64,128,768]{2,1,0:T(8,128)(2,1)} %weight_ref.3, bf16[256,64,196]{2,1,0:T(8,128)(2,1)} %copy.123.pix_ref), custom_call_target="tpu_custom_call" | custom-call | tf_op jit(solution)/shard_map/embed/pallas_call | solution.py:140
  73.6 20.5 %collective-permute-done.2 = bf16[3,208,768]{2,1,0:T(8,128)(2,1)} collective-permute-done((bf16[3,208,768]{2,1,0:T(8,128)(2,1)}, bf16[3,208,768]{2,1,0:T(8,128)(2,1)}, u32[]{:S(2)}, u32[]{:S(2)}) %collective-permute-start.2) | collective-permute-done | bytes 958496 | tf_op jit(solution)/shard_map/ppermute | solution.py:409
  104.1 5.5 convolution_convert_fusion.3
  109.6 9.2 %reshape.352 = bf16[3,196,3,12,64]{4,3,2,1,0:T(8,128)(2,1)} reshape(bf16[588,2304]{1,0:T(8,128)(2,1)} %convolution_convert_fusion.3) | data formatting | bytes 5419008 | tf_op jit(solution)/shard_map/reshape | solution.py:605
  118.8 6.6 fusion.84
  125.5 4.2 copy.161
  129.7 4.2 copy.160
  133.9 4.3 copy.162
  155.4 5.9 fusion.78
  161.4 20.7 %add_convert_fusion = (bf16[588,3072]{1,0:T(8,128)(2,1)S(1)}, f32[588,3072]{1,0:T(8,128)}) fusion(f32[588,3072]{1,0:T(8,128)S(1)} %fusion.78, bf16[588,768]{1,0:T(8,128)(2,1)S(1)} %copy-done.15, bf16[3072,768]{1,0:T(8,128)(2,1)S(1)} %bitcast.177), kind=kOutput, calls=%fused_computation.6 | convolution fusion | flops 2904588288 | bytes 23685120 | tf_op jit(solution)/shard_map/rd,fd->rf/dot_general | solution.py:631
  195.1 4.2 copy.131
  199.3 5.0 convolution_bitcast_fusion
  204.3 5.3 multiply_reduce_fusion
  215.3 5.6 copy.136
  220.9 9.8 %convert_element_type.223 = bf16[588,2304]{0,1:T(8,128)(2,1)} reshape(bf16[3,196,3,12,64]{1,0,4,3,2:T(4,128)(2,1)} %copy.136) | data formatting | bytes 5419008 | tf_op jit(solution)/shard_map/convert_element_type | solution.py:675
  230.7 6.1 multiply_reduce_fusion.4
  251.5 16.4 %collective-permute-done.4 = bf16[3,208,768]{2,1,0:T(8,128)(2,1)} collective-permute-done((bf16[3,208,768]{2,1,0:T(8,128)(2,1)}, bf16[3,208,768]{2,1,0:T(8,128)(2,1)}, u32[]{:S(2)}, u32[]{:S(2)}) %collective-permute-start.4) | collective-permute-done | bytes 958496 | tf_op jit(solution)/shard_map/ppermute | solution.py:409
  276.3 33.7 %embed_back.1 = (bf16[256,64,196]{2,1,0:T(8,128)(2,1)}, bf16[64,32,768]{2,1,0:T(8,128)(2,1)}, f32[32,128]{1,0:T(8,128)}) custom-call(s32[12]{0:T(128)} %bitcast.173, s32[256]{0:T(256)} %bitcast.171, bf16[12,208,768]{2,1,0:T(8,128)(2,1)} %pad_maximum_fusion.grad_ref, bf16[32,64,768]{2,1,0:T(8,128)(2,1)} %get-tuple-element.28.table_ref, ...), custom_call_target="tpu_custom_call" | custom-call | tf_op jit(solution)/shard_map/embed_back/pallas_call | solution.py:303
  315.6 5.1 convolution_convert_fusion.2
  331.8 6.7 %convolution_convert_fusion.1 = bf16[768,3072]{1,0:T(8,128)(2,1)S(1)} fusion(bf16[588,3072]{1,0:T(8,128)(2,1)} %copy-done.78, f32[588,768]{1,0:T(8,128)} %copy-done.10, f32[768]{0:T(1024)S(1)} %copy-done.77, f32[768]{0:T(1024)S(1)} %copy-done.66, f32[588]{0:T(1024)S(1)} %copy-done.47, f32[588]{0:T(1024)S(1)} %broadcast_multiply_fusion.1), kind=kOutput, calls=%fused_computation.24 | convolution fusion | flops 2779149312 | bytes 10148448 | tf_op jit(solution)/shard_map/rd,rf->df/dot_general | solution.py:635
  347.2 4.4 add_convert_fusion.2
  351.9 7.1 %multiply_convert_fusion.1 = bf16[588,3072]{1,0:T(8,128)(2,1)S(1)} fusion(f32[588,3072]{1,0:T(8,128)} %get-tuple-element.138, f32[588,3072]{1,0:T(8,128)} %copy-done.9), kind=kLoop, calls=%fused_computation.7 | loop fusion | flops 5419008 | bytes 18063360 | tf_op jit(solution)/shard_map/convert_element_type | solution.py:625
  359.0 4.2 convolution_convert_fusion
  369.1 8.0 %add_convert_fusion.6 = bf16[588,768]{1,0:T(8,128)(2,1)} fusion(f32[588,768]{1,0:T(8,128)} %copy-done.10, bf16[588,3072]{1,0:T(8,128)(2,1)} %copy-done.18, bf16[3072,768]{1,0:T(8,128)(2,1)} %param.46), kind=kOutput, calls=%fused_computation.51 | convolution fusion | flops 2775435264 | bytes 11040768 | tf_op jit(solution)/shard_map/dot_general | solution.py:626
  384.0 42.1 %psum.7 = f32[62,128]{1,0:T(8,128)} all-reduce(f32[62,128]{1,0:T(8,128)} %pad_maximum_fusion.3), channel_id=1, replica_groups=mesh['band'=8,'rows'=4] {'band','rows'}, use_global_device_ids=true, to_apply=%region_23.24 | all-reduce | flops 7936 | bytes 63488 | tf_op jit(solution)/shard_map/psum | solution.py:711
  433.2 4.5 add_convert_fusion.1
  441.1 13.1 %copy.146 = bf16[256,64,196]{0,1,2:T(8,128)(2,1)} copy(bf16[256,64,196]{2,1,0:T(8,128)(2,1)} %get-tuple-element.97) | data formatting | bytes 12845056
  482.7 5.3 all-to-all-start
  496.2 78.6 %reduce-scatter.12.cloned.1.call-done = bf16[96,1536]{1,0:T(8,128)(2,1)} async-done(((bf16[768,1536]{1,0:T(8,128)(2,1)}), bf16[96,1536]{1,0:T(8,128)(2,1)}) %reduce-scatter.12.cloned.1.call-update) | async-done | bytes 294928 | tf_op jit(solution)/shard_map/reduce_scatter | solution.py:456
  578.1 68.4 %reduce-scatter.14.cloned.1.call-done = bf16[384,384]{1,0:T(8,128)(2,1)} async-done(((bf16[3072,384]{1,0:T(8,128)(2,1)}), bf16[384,384]{1,0:T(8,128)(2,1)}) %reduce-scatter.14.cloned.1.call-update) | async-done | bytes 294928 | tf_op jit(solution)/shard_map/reduce_scatter | solution.py:456
  649.2 5.2 collective-permute-done.16
  (342 shorter events, 192.9 us)
Async XLA Ops:
  7.2 96.9 %copy-start = (bf16[768,2304]{1,0:T(8,128)(2,1)S(1)}, bf16[768,2304]{1,0:T(8,128)(2,1)}, u32[]{:S(2)}) copy-start(bf16[768,2304]{1,0:T(8,128)(2,1)} %param.41) | copy-start | bytes 10616836
  7.2 360.4 %reduce-scatter.10.cloned.1.call-start = ((), (), s32[]{:S(2)}) async-start(), calls=%async_computation.8 | async-start | bytes 663552 | tf_op jit(solution)/shard_map/reduce_scatter | solution.py:456
  63.7 3.0 collective-permute-start.1
  64.2 9.4 %collective-permute-start = (bf16[3,208,768]{2,1,0:T(8,128)(2,1)}, bf16[3,208,768]{2,1,0:T(8,128)(2,1)}, u32[]{:S(2)}, u32[]{:S(2)}) collective-permute-start(bf16[3,208,768]{2,1,0:T(8,128)(2,1)} %get-tuple-element.148), channel_id=1, source_target_pairs={{0,1},{1,0},{2,3},{3,2},{4,5},{5,4},{6,7},{7,6},{8,9},{9,8},{10,11... | collective-permute-start | bytes 2875400 | tf_op jit(solution)/shard_map/ppermute | solution.py:405
  69.3 24.7 %collective-permute-start.2 = (bf16[3,208,768]{2,1,0:T(8,128)(2,1)}, bf16[3,208,768]{2,1,0:T(8,128)(2,1)}, u32[]{:S(2)}, u32[]{:S(2)}) collective-permute-start(bf16[3,208,768]{2,1,0:T(8,128)(2,1)} %add_convert_fusion.4), channel_id=1, source_target_pairs={{0,2},{2,0},{1,3},{3,1},{4,6},{6,4},{5,7},{7,5},{8,10},{10,8},{9,1... | collective-permute-start | bytes 2875400 | tf_op jit(solution)/shard_map/ppermute | solution.py:409
  154.9 31.1 %copy-start.10 = (f32[588,768]{1,0:T(8,128)}, f32[588,768]{1,0:T(8,128)S(1)}, u32[]{:S(2)}) copy-start(f32[588,768]{1,0:T(8,128)S(1)} %get-tuple-element.174) | copy-start | bytes 5419012
  155.3 30.7 %copy-start.46 = (f32[588]{0:T(1024)}, f32[588]{0:T(1024)S(1)}, u32[]{:S(2)}) copy-start(f32[588]{0:T(1024)S(1)} %fusion.62) | copy-start | bytes 7060
  155.4 26.8 %slice-start.2 = ((s8[4718592]{0:T(1024)(128)(4,1)}), s8[4194304]{0:T(1024)(128)(4,1)S(1)}, s32[]{:S(2)}) async-start(s8[4718592]{0:T(1024)(128)(4,1)} %bitcast.174), calls=%async_computation.13 | async-start | bytes 8388608
  161.3 20.8 %copy-start.9 = (f32[588,3072]{1,0:T(8,128)}, f32[588,3072]{1,0:T(8,128)S(1)}, u32[]{:S(2)}) copy-start(f32[588,3072]{1,0:T(8,128)S(1)} %fusion.78) | copy-start | bytes 21676036
  161.3 20.8 %slice-start.3 = ((s8[4718592]{0:T(1024)(128)(4,1)}), s8[524288]{0:T(1024)(128)(4,1)S(1)}, s32[]{:S(2)}) async-start(s8[4718592]{0:T(1024)(128)(4,1)} %bitcast.174), calls=%async_computation.14 | async-start | bytes 1048576
  244.8 23.1 %collective-permute-start.4 = (bf16[3,208,768]{2,1,0:T(8,128)(2,1)}, bf16[3,208,768]{2,1,0:T(8,128)(2,1)}, u32[]{:S(2)}, u32[]{:S(2)}) collective-permute-start(bf16[3,208,768]{2,1,0:T(8,128)(2,1)} %pad.19), channel_id=1, source_target_pairs={{0,2},{2,0},{1,3},{3,1},{4,6},{6,4},{5,7},{7,5},{8,10},{10,8},{9,1... | collective-permute-start | bytes 2875400 | tf_op jit(solution)/shard_map/ppermute | solution.py:409
  246.6 23.6 %collective-permute-start.3 = (bf16[3,208,768]{2,1,0:T(8,128)(2,1)}, bf16[3,208,768]{2,1,0:T(8,128)(2,1)}, u32[]{:S(2)}, u32[]{:S(2)}) collective-permute-start(bf16[3,208,768]{2,1,0:T(8,128)(2,1)} %pad.19), channel_id=1, source_target_pairs={{0,1},{1,0},{2,3},{3,2},{4,5},{5,4},{6,7},{7,6},{8,9},{9,8},{10,11... | collective-permute-start | bytes 2875400 | tf_op jit(solution)/shard_map/ppermute | solution.py:405
  251.0 16.9 %collective-permute-start.9 = (bf16[768,384]{1,0:T(8,128)(2,1)}, bf16[768,384]{1,0:T(8,128)(2,1)}, u32[]{:S(2)}, u32[]{:S(2)}) collective-permute-start(bf16[768,384]{1,0:T(8,128)(2,1)} %constant_dynamic-slice_fusion.2), channel_id=1, source_target_pairs={{0,1},{1,0},{2,3},{3,2},{4,5},{5,4},{6,7},{7,6},{8,9},{9,8},{10,11... | collective-permute-start | bytes 1769480 | tf_op jit(solution)/shard_map/ppermute | solution.py:405
  267.9 4.1 collective-permute-start.5
  270.1 206.8 %reduce-scatter.6.cloned.1.call-start = ((), (), s32[]{:S(2)}) async-start(), calls=%async_computation.6 | async-start | bytes 3538944 | tf_op jit(solution)/shard_map/reduce_scatter | solution.py:719
  310.0 183.5 %reduce-scatter.8.cloned.1.call-start = ((), (), s32[]{:S(2)}) async-start(), calls=%async_computation.7 | async-start | bytes 1990656 | tf_op jit(solution)/shard_map/reduce_scatter | solution.py:456
  323.9 4.2 collective-permute-start.6
  331.7 243.1 %reduce-scatter.12.cloned.1.call-start = ((), (), s32[]{:S(2)}) async-start(), calls=%async_computation.9 | async-start | bytes 2654208 | tf_op jit(solution)/shard_map/reduce_scatter | solution.py:456
  342.3 4.9 collective-permute-start.12
  351.6 294.9 %reduce-scatter.14.cloned.1.call-start = ((), (), s32[]{:S(2)}) async-start(), calls=%async_computation.10 | async-start | bytes 2654208 | tf_op jit(solution)/shard_map/reduce_scatter | solution.py:456
  367.2 10.6 %copy-start.45 = (f32[768]{0:T(1024)S(1)}, f32[768]{0:T(1024)}, u32[]{:S(2)}) copy-start(f32[768]{0:T(1024)} %get-tuple-element.144) | copy-start | bytes 9220
  367.2 66.0 %collective-permute-start.15 = (bf16[3072,384]{1,0:T(8,128)(2,1)}, bf16[3072,384]{1,0:T(8,128)(2,1)}, u32[]{:S(2)}, u32[]{:S(2)}) collective-permute-start(bf16[3072,384]{1,0:T(8,128)(2,1)} %constant_dynamic-slice_fusion), channel_id=1, source_target_pairs={{0,1},{1,0},{2,3},{3,2},{4,5},{5,4},{6,7},{7,6},{8,9},{9,8},{10,11... | collective-permute-start | bytes 7077896 | tf_op jit(solution)/shard_map/ppermute | solution.py:405
  367.6 13.5 %collective-permute-start.10 = (bf16[96,384]{1,0:T(8,128)(2,1)}, bf16[96,384]{1,0:T(8,128)(2,1)}, u32[]{:S(2)}, u32[]{:S(2)}) collective-permute-start(bf16[96,384]{1,0:T(8,128)(2,1)} %reduce-scatter.10.cloned.1.call-done), channel_id=1, source_target_pairs={{0,2},{2,0},{1,3},{3,1},{4,6},{6,4},{5,7},{7,5},{8,10},{10,8},{9,1... | collective-permute-start | bytes 221192 | tf_op jit(solution)/shard_map/ppermute | solution.py:409
  382.7 86.6 %collective-permute-start.11 = (bf16[96,384]{1,0:T(8,128)(2,1)}, bf16[96,384]{1,0:T(8,128)(2,1)}, u32[]{:S(2)}, u32[]{:S(2)}) collective-permute-start(bf16[96,384]{1,0:T(8,128)(2,1)} %add_convert_fusion.14), channel_id=1, source_target_pairs={{0,1},{1,0},{2,3},{3,2},{4,5},{5,4},{6,7},{7,6},{8,9},{9,8},{10,11... | collective-permute-start | bytes 221192 | tf_op jit(solution)/shard_map/ppermute | solution.py:405
  454.2 16.8 %copy-start.34 = (f32[32,64]{1,0:T(8,128)S(1)}, f32[32,64]{1,0:T(8,128)}, u32[]{:S(2)}) copy-start(f32[32,64]{1,0:T(8,128)} %copy-done.33) | copy-start | bytes 24580
  482.7 177.4 %all-to-all-start = ((bf16[8,128,768]{2,0,1:T(8,128)(2,1)}), bf16[8,128,768]{2,0,1:T(8,128)(2,1)}, u32[]{:S(2)}, u32[]{:S(2)}) async-start(bf16[8,128,768]{2,0,1:T(8,128)(2,1)} %copy.138), calls=%async_computation.1 | async-start | bytes 3145728 | tf_op jit(solution)/shard_map/all_to_all | solution.py:723
  493.5 82.8 %collective-permute-start.7 = (bf16[96,1152]{1,0:T(8,128)(2,1)}, bf16[96,1152]{1,0:T(8,128)(2,1)}, u32[]{:S(2)}, u32[]{:S(2)}) collective-permute-start(bf16[96,1152]{1,0:T(8,128)(2,1)} %reduce-scatter.8.cloned.1.call-done), channel_id=1, source_target_pairs={{0,2},{2,0},{1,3},{3,1},{4,6},{6,4},{5,7},{7,5},{8,10},{10,8},{9,1... | collective-permute-start | bytes 663560 | tf_op jit(solution)/shard_map/ppermute | solution.py:409
  574.9 73.1 %collective-permute-start.13 = (bf16[96,1536]{1,0:T(8,128)(2,1)}, bf16[96,1536]{1,0:T(8,128)(2,1)}, u32[]{:S(2)}, u32[]{:S(2)}) collective-permute-start(bf16[96,1536]{1,0:T(8,128)(2,1)} %reduce-scatter.12.cloned.1.call-done), channel_id=1, source_target_pairs={{0,2},{2,0},{1,3},{3,1},{4,6},{6,4},{5,7},{7,5},{8,10},{10,8},{9,1... | collective-permute-start | bytes 884744 | tf_op jit(solution)/shard_map/ppermute | solution.py:409
  578.1 77.4 %collective-permute-start.8 = (bf16[96,1152]{1,0:T(8,128)(2,1)}, bf16[96,1152]{1,0:T(8,128)(2,1)}, u32[]{:S(2)}, u32[]{:S(2)}) collective-permute-start(bf16[96,1152]{1,0:T(8,128)(2,1)} %add_convert_fusion.13), channel_id=1, source_target_pairs={{0,1},{1,0},{2,3},{3,2},{4,5},{5,4},{6,7},{7,6},{8,9},{9,8},{10,11... | collective-permute-start | bytes 663560 | tf_op jit(solution)/shard_map/ppermute | solution.py:405
  646.5 7.9 %collective-permute-start.16 = (bf16[384,384]{1,0:T(8,128)(2,1)}, bf16[384,384]{1,0:T(8,128)(2,1)S(1)}, u32[]{:S(2)}, u32[]{:S(2)}) collective-permute-start(bf16[384,384]{1,0:T(8,128)(2,1)} %reduce-scatter.14.cloned.1.call-done), channel_id=1, source_target_pairs={{0,2},{2,0},{1,3},{3,1},{4,6},{6,4},{5,7},{7,5},{8,10},{10,8},{9,1... | collective-permute-start | bytes 884744 | tf_op jit(solution)/shard_map/ppermute | solution.py:409
  649.1 9.8 %collective-permute-start.14 = (bf16[96,1536]{1,0:T(8,128)(2,1)S(1)}, bf16[96,1536]{1,0:T(8,128)(2,1)S(1)}, u32[]{:S(2)}, u32[]{:S(2)}) collective-permute-start(bf16[96,1536]{1,0:T(8,128)(2,1)S(1)} %add_convert_fusion.12), channel_id=1, source_target_pairs={{0,1},{1,0},{2,3},{3,2},{4,5},{5,4},{6,7},{7,6},{8,9},{9,8},{10,11... | collective-permute-start | bytes 884744 | tf_op jit(solution)/shard_map/ppermute | solution.py:405
  655.5 2.4 collective-permute-start.17
  (77 other events, 337.3 us)
Sparse Core Ops, SparseCore 0:
  270.3 63.4 reduce-scatter.9
  337.7 74.1 reduce-scatter.5
  415.8 65.2 reduce-scatter.7
  485.1 89.7 reduce-scatter.11
  578.2 68.2 reduce-scatter.13

commit v2 on v1

--- a/solution.py
+++ b/solution.py
@@ -12,6 +12,8 @@
 STEPS = 8
 QUAD = 4
 LANES = 128
+EPSILON = 1e-06
+ROW_STEP = 48
 
 
 def pad_rows(rows):
@@ -333,6 +335,327 @@
     )(counts, band_waves, grads, table, sums, pixels, kernel_weight)
 
 
+over_last = (((1,), (1,)), ((), ()))
+over_first = (((0,), (0,)), ((), ()))
+
+
+def times(left, right):
+    return jnp.dot(left, right, preferred_element_type=jnp.float32)
+
+
+def times_turned(left, right):
+    return lax.dot_general(left, right, over_last, preferred_element_type=jnp.float32)
+
+
+def turned_times(left, right):
+    return lax.dot_general(left, right, over_first, preferred_element_type=jnp.float32)
+
+
+def norm_parts(values):
+    centered = values - jnp.mean(values, axis=-1, keepdims=True)
+    variance = jnp.mean(centered * centered, axis=-1, keepdims=True)
+    scale = lax.rsqrt(variance + EPSILON)
+    return centered * scale, scale
+
+
+def norm_backward(values, slope, gain):
+    unit, scale = norm_parts(values)
+    inner = slope * gain
+    mean = jnp.mean(inner, axis=-1, keepdims=True)
+    along = jnp.mean(inner * unit, axis=-1, keepdims=True)
+    return scale * (inner - mean - unit * along), slope * unit
+
+
+def by_rows(total, fn):
+    def part(i, carry):
+        fn(pl.ds(pl.multiple_of(i * ROW_STEP, ROW_STEP), ROW_STEP))
+        return carry
+
+    lax.fori_loop(0, total // ROW_STEP, part, 0)
+
+
+def attend_kernel(
+    near_ref, far_ref, bias_ref, gain_ref, shift_ref, qkv_ref, proj_ref, mid_gain_ref, mid_shift_ref,
+    x_ref, normed_ref, projected_ref, probs_ref, mixed_ref, middle_ref, normed_mid_ref,
+    *, padded, patches,
+):
+    rows, width = x_ref.shape
+    head = width // HEADS
+    images, pairs = rows // padded, HEADS // 2
+
+    def first(r):
+        x = near_ref[r, :] + far_ref[r, :].astype(jnp.float32) + bias_ref[...]
+        x_ref[r, :] = x
+        normed_ref[r, :] = (norm_parts(x)[0] * gain_ref[...] + shift_ref[...]).astype(jnp.bfloat16)
+
+    by_rows(rows, first)
+    for part in range(3):
+        columns = slice(part * width, (part + 1) * width)
+        projected_ref[:, columns] = times(normed_ref[...], qkv_ref[:, columns]).astype(jnp.bfloat16)
+    lane = lax.broadcasted_iota(jnp.int32, (padded, LANES), 1)
+    key = lax.broadcasted_iota(jnp.int32, (padded, padded), 1)
+    factor = jnp.bfloat16(1.0 / math.sqrt(head))
+
+    def pair_of(index, carry):
+        image, pair = index // pairs, index % pairs
+        r = pl.ds(pl.multiple_of(image * padded, padded), padded)
+
+        def columns(part):
+            return pl.ds(pl.multiple_of(part * width + pair * LANES, LANES), LANES)
+
+        queries, keys, values = (projected_ref[r, columns(part)] for part in range(3))
+        found = []
+        for h in range(2):
+            mine = (lane // head) == h
+            scores = times_turned(jnp.where(mine, queries * factor, jnp.zeros_like(queries)), keys)
+            scores = jnp.where(key < patches, scores, -1e30)
+            raised = jnp.exp(scores - jnp.max(scores, axis=-1, keepdims=True))
+            probs = raised * (1.0 / jnp.sum(raised, axis=-1, keepdims=True))
+            low = probs.astype(jnp.bfloat16)
+            probs_ref[index * 2 + h] = low
+            found.append(times(low, values))
+        mixed_ref[r, pl.ds(pl.multiple_of(pair * LANES, LANES), LANES)] = jnp.where(
+            lane < head, found[0], found[1]
+        ).astype(jnp.bfloat16)
+        return carry
+
+    lax.fori_loop(0, images * pairs, pair_of, 0)
+    middle_ref[...] = times(mixed_ref[...], proj_ref[...])
+
+    def last(r):
+        middle = middle_ref[r, :] + x_ref[r, :]
+        middle_ref[r, :] = middle
+        normed_mid_ref[r, :] = (
+            norm_parts(middle)[0] * mid_gain_ref[...] + mid_shift_ref[...]
+        ).astype(jnp.bfloat16)
+
+    by_rows(rows, last)
+
+
+def whole(*shape):
+    return pl.BlockSpec(shape, lambda *index: (0,) * len(shape))
+
+
+def attend_call(near, far, bias, gain, shift, qkv, proj, mid_gain, mid_shift, padded, patches):
+    rows, width = near.shape
+    images = rows // padded
+    row = lambda v: v.reshape(1, width)
+    shapes = [
+        ((rows, width), jnp.float32),
+        ((rows, width), jnp.bfloat16),
+        ((rows, 3 * width), jnp.bfloat16),
+        ((images * HEADS, padded, padded), jnp.bfloat16),
+        ((rows, width), jnp.bfloat16),
+        ((rows, width), jnp.float32),
+        ((rows, width), jnp.bfloat16),
+    ]
+    return pl.pallas_call(
+        functools.partial(attend_kernel, padded=padded, patches=patches),
+        out_shape=[jax.ShapeDtypeStruct(*s) for s in shapes],
+        compiler_params=pltpu.CompilerParams(vmem_limit_bytes=VMEM_LIMIT),
+        name="attend",
+    )(near, far, row(bias), row(gain), row(shift), qkv, proj, row(mid_gain), row(mid_shift))
+
+
+def mlp_kernel(
+    normed_ref, middle_ref, cot_ref, gain_ref, up_ref, down_ref,
+    out_ref, grad_ref, low_ref, down_grad_ref, up_grad_ref, gain_grad_ref, shift_grad_ref,
+    result_ref, slope_ref, wide_ref, back_ref, active_ref, grad_up_ref,
+):
+    step = pl.program_id(0)
+    rows = normed_ref.shape[0]
+    wide_ref[...] = times(normed_ref[...], up_ref[...])
+    back_ref[...] = times_turned(cot_ref[...], down_ref[...])
+
+    def middle_part(r):
+        x = wide_ref[r, :]
+        below = 0.5 * (1.0 + lax.erf(x * math.sqrt(0.5)))
+        density = jnp.exp(-0.5 * x * x) * (1.0 / math.sqrt(2.0 * math.pi))
+        active_ref[r, :] = (x * below).astype(jnp.bfloat16)
+        grad_up_ref[r, :] = (back_ref[r, :] * (below + x * density)).astype(jnp.bfloat16)
+
+    by_rows(rows, middle_part)
+    down_grad_ref[...] = turned_times(active_ref[...], cot_ref[...]).astype(jnp.bfloat16)
+    up_grad_ref[0] = turned_times(normed_ref[...], grad_up_ref[...]).astype(jnp.bfloat16)
+
+    @pl.when(step == 0)
+    def _():
+        result_ref[...] = times(active_ref[...], down_ref[...])
+        slope_ref[...] = times_turned(grad_up_ref[...], up_ref[...])
+
+    @pl.when(step > 0)
+    def _():
+        result_ref[...] += times(active_ref[...], down_ref[...])
+        slope_ref[...] += times_turned(grad_up_ref[...], up_ref[...])
+
+    @pl.when(step == pl.num_programs(0) - 1)
+    def _():
+        gain_grad_ref[...] = jnp.zeros_like(gain_grad_ref)
+        shift_grad_ref[...] = jnp.zeros_like(shift_grad_ref)
+
+        def last(r):
+            middle, slope = middle_ref[r, :], slope_ref[r, :]
+            out_ref[r, :] = (middle + result_ref[r, :]).astype(jnp.bfloat16)
+            back, terms = norm_backward(middle, slope, gain_ref[...])
+            grad = cot_ref[r, :].astype(jnp.float32) + back
+            grad_ref[r, :] = grad
+            low_ref[r, :] = grad.astype(jnp.bfloat16)
+            gain_grad_ref[...] += jnp.sum(terms, axis=0, keepdims=True)
+            shift_grad_ref[...] += jnp.sum(slope, axis=0, keepdims=True)
+
+        by_rows(rows, last)
+
+
+def mlp_call(normed, middle, cot, gain, up, down):
+    rows, width = middle.shape
+    hidden = up.shape[1]
+    steps = hidden // width
+    f32, bf16 = jnp.float32, jnp.bfloat16
+    return pl.pallas_call(
+        mlp_kernel,
+        grid=(steps,),
+        in_specs=[
+            whole(rows, width),
+            whole(rows, width),
+            whole(rows, width),
+            whole(1, width),
+            pl.BlockSpec((width, width), lambda j: (0, j)),
+            pl.BlockSpec((width, width), lambda j: (j, 0)),
+        ],
+        out_specs=[
+            whole(rows, width),
+            whole(rows, width),
+            whole(rows, width),
+            pl.BlockSpec((width, width), lambda j: (j, 0)),
+            pl.BlockSpec((1, width, width), lambda j: (j, 0, 0)),
+            whole(1, width),
+            whole(1, width),
+        ],
+        out_shape=[
+            jax.ShapeDtypeStruct((rows, width), bf16),
+            jax.ShapeDtypeStruct((rows, width), f32),
+            jax.ShapeDtypeStruct((rows, width), bf16),
+            jax.ShapeDtypeStruct((hidden, width), bf16),
+            jax.ShapeDtypeStruct((steps, width, width), bf16),
+            jax.ShapeDtypeStruct((1, width), f32),
+            jax.ShapeDtypeStruct((1, width), f32),
+        ],
+        scratch_shapes=[pltpu.VMEM((rows, width), t) for t in (f32, f32, f32, f32, bf16, bf16)],
+        compiler_params=pltpu.CompilerParams(vmem_limit_bytes=VMEM_LIMIT),
+        name="mlp",
+    )(normed, middle, cot, gain.reshape(1, width), up, down)
+
+
+def attend_back_kernel(
+    low_ref, grad_ref, x_ref, projected_ref, probs_ref, gain_ref, qkv_ref, proj_ref,
+    grad_x_ref, grad_projected_ref, bias_grad_ref, gain_grad_ref, shift_grad_ref,
+    mixed_grad_ref, slope_ref,
+    *, padded,
+):
+    rows, width = x_ref.shape
+    head = width // HEADS
+    images, pairs = rows // padded, HEADS // 2
+    mixed_grad_ref[...] = times_turned(low_ref[...], proj_ref[...]).astype(jnp.bfloat16)
+    lane = lax.broadcasted_iota(jnp.int32, (padded, LANES), 1)
+    factor = jnp.bfloat16(1.0 / math.sqrt(head))
+
+    def pair_of(index, carry):
+        image, pair = index // pairs, index % pairs
+        r = pl.ds(pl.multiple_of(image * padded, padded), padded)
+
+        def columns(part):
+            return pl.ds(pl.multiple_of(part * width + pair * LANES, LANES), LANES)
+
+        queries, keys, values = (projected_ref[r, columns(part)] for part in range(3))
+        queries, keys = queries * factor, keys * factor
+        grads = mixed_grad_ref[r, columns(0)]
+        found = [], [], []
+        for h in range(2):
+            mine = (lane // head) == h
+            low = probs_ref[index * 2 + h]
+            probs = low.astype(jnp.float32)
+            grad_probs = times_turned(jnp.where(mine, grads, jnp.zeros_like(grads)), values)
+            scaled = grad_probs * probs
+            total = jnp.sum(scaled, axis=-1, keepdims=True)
+            grad_scores = (scaled - probs * total).astype(jnp.bfloat16)
+            found[0].append(times(grad_scores, keys))
+            found[1].append(turned_times(grad_scores, queries))
+            found[2].append(turned_times(low, grads))
+        for part in range(3):
+            grad_projected_ref[r, columns(part)] = jnp.where(
+                lane < head, found[part][0], found[part][1]
+            ).astype(jnp.bfloat16)
+        return carry
+
+    lax.fori_loop(0, images * pairs, pair_of, 0)
+    slope_ref[...] = times_turned(grad_projected_ref[:, :width], qkv_ref[:, :width])
+    for part in range(1, 3):
+        columns = slice(part * width, (part + 1) * width)
+        slope_ref[...] += times_turned(grad_projected_ref[:, columns], qkv_ref[:, columns])
+    for ref in (bias_grad_ref, gain_grad_ref, shift_grad_ref):
+        ref[...] = jnp.zeros_like(ref)
+
+    def last(r):
+        slope = slope_ref[r, :]
+        back, terms = norm_backward(x_ref[r, :], slope, gain_ref[...])
+        grad = grad_ref[r, :] + back
+        grad_x_ref[r, :] = grad.astype(jnp.bfloat16)
+        bias_grad_ref[...] += jnp.sum(grad, axis=0, keepdims=True)
+        gain_grad_ref[...] += jnp.sum(terms, axis=0, keepdims=True)
+        shift_grad_ref[...] += jnp.sum(slope, axis=0, keepdims=True)
+
+    by_rows(rows, last)
+
+
+def attend_back_call(low, grad, x, projected, probs, gain, qkv, proj, padded):
+    rows, width = x.shape
+    f32, bf16 = jnp.float32, jnp.bfloat16
+    shapes = [
+        ((rows, width), bf16),
+        ((rows, 3 * width), bf16),
+        ((1, width), f32),
+        ((1, width), f32),
+        ((1, width), f32),
+    ]
+    return pl.pallas_call(
+        functools.partial(attend_back_kernel, padded=padded),
+        out_shape=[jax.ShapeDtypeStruct(*s) for s in shapes],
+        scratch_shapes=[pltpu.VMEM((rows, width), bf16), pltpu.VMEM((rows, width), f32)],
+        compiler_params=pltpu.CompilerParams(vmem_limit_bytes=VMEM_LIMIT),
+        name="attend_back",
+    )(low, grad, x, projected, probs, gain.reshape(1, width), qkv, proj)
+
+
+def attend_weights_kernel(normed_ref, mixed_ref, grad_projected_ref, low_ref, out_ref):
+    step = pl.program_id(0)
+
+    @pl.when(step < 3)
+    def _():
+        out_ref[0] = turned_times(normed_ref[...], grad_projected_ref[...]).astype(jnp.bfloat16)
+
+    @pl.when(step == 3)
+    def _():
+        out_ref[0] = turned_times(mixed_ref[...], low_ref[...]).astype(jnp.bfloat16)
+
+
+def attend_weights_call(normed, mixed, grad_projected, low):
+    rows, width = normed.shape
+    return pl.pallas_call(
+        attend_weights_kernel,
+        grid=(4,),
+        in_specs=[
+            whole(rows, width),
+            whole(rows, width),
+            pl.BlockSpec((rows, width), lambda j: (0, jnp.minimum(j, 2))),
+            whole(rows, width),
+        ],
+        out_specs=pl.BlockSpec((1, width, width), lambda j: (j, 0, 0)),
+        out_shape=jax.ShapeDtypeStruct((4, width, width), jnp.bfloat16),
+        compiler_params=pltpu.CompilerParams(vmem_limit_bytes=VMEM_LIMIT),
+        name="attend_weights",
+    )(normed, mixed, grad_projected, low)
+
+
 HEADS = 12
 WD = 128
 WHEADS = 4
@@ -349,14 +672,6 @@
     centered = values - jnp.mean(values, axis=-1, keepdims=True)
     variance = jnp.mean(centered * centered, axis=-1, keepdims=True)
     return centered * lax.rsqrt(variance + epsilon) * norm_gain + norm_shift
-
-
-def block_norm(values, norm_gain, norm_shift):
-    return layer_norm(values, norm_gain, norm_shift, 1e-06)
-
-
-def exact_gelu(values):
-    return jax.nn.gelu(values, approximate=False)
 
 
 def wave_embed(wavelengths):
@@ -425,7 +740,7 @@
 
     far = add_wide(block(1 - chip, core), swap_core(block(1 - chip, 1 - core)))
     near = add_wide(block(chip, core), swap_core(block(chip, 1 - core)))
-    return near + swap_chip(far.astype(jnp.bfloat16)).astype(jnp.float32)
+    return near, swap_chip(far.astype(jnp.bfloat16))
 
 
 def rows_gather(own):
@@ -446,21 +761,67 @@
     )
 
 
-def weight_reduce(grad):
-    core = lax.axis_index("rows") % 2
-    half = grad.shape[1] // 2
-    low = grad.astype(jnp.bfloat16)
-    kept = lax.dynamic_slice_in_dim(low, core * half, half, 1)
-    sent = lax.dynamic_slice_in_dim(low, (1 - core) * half, half, 1)
-    pair = add_wide(kept, swap_core(sent)).astype(jnp.bfloat16)
-    part = lax.psum_scatter(pair, "band", scatter_dimension=0, tiled=True)
-    whole = add_wide(part, swap_chip(part)).astype(jnp.bfloat16)
-    other = swap_core(whole)
+def swap_band(array, bit):
+    count = lax.axis_size("band")
+    return lax.ppermute(array, "band", [(i, i ^ (1 << bit)) for i in range(count)])
+
+
+def halve(array, axis, bit, swap):
+    half = array.shape[axis] // 2
+    kept = lax.dynamic_slice_in_dim(array, bit * half, half, axis)
+    sent = lax.dynamic_slice_in_dim(array, (1 - bit) * half, half, axis)
+    return add_wide(kept, swap(sent)).astype(array.dtype)
+
+
+def band_halve(array, axis):
+    place = lax.axis_index("band")
+    for bit in range(lax.axis_size("band").bit_length() - 1):
+        shape = array.shape
+        split = (*shape[:axis], shape[axis] // 2, 2, *shape[axis + 1 :])
+        array = halve(
+            array.reshape(split),
+            axis + 1,
+            (place >> bit) & 1,
+            functools.partial(swap_band, bit=bit),
+        )
+        array = array.reshape(*shape[:axis], shape[axis] // 2, *shape[axis + 1 :])
+    return array
+
+
+def join(own, other, bit, axis):
     return jnp.where(
-        core == 0,
-        jnp.concatenate([whole, other], axis=1),
-        jnp.concatenate([other, whole], axis=1),
-    ).astype(jnp.float32)
+        bit == 0,
+        jnp.concatenate([own, other], axis=axis),
+        jnp.concatenate([other, own], axis=axis),
+    )
+
+
+def weight_reduce(grad, chip_first):
+    place = lax.axis_index("rows")
+    chip, core = place // 2, place % 2
+    parts, rows, width = grad.shape
+    bands = lax.axis_size("band")
+    array = halve(grad.reshape(parts, bands, rows // bands, width), 3, core, swap_core)
+    if chip_first:
+        array = halve(array, 2, chip, swap_chip)
+    array = band_halve(array, 1)[:, 0]
+    if chip_first:
+        array = join(array, swap_chip(array), chip, 1)
+    else:
+        array = add_wide(array, swap_chip(array)).astype(array.dtype)
+    return join(array, swap_core(array), core, 2).astype(jnp.float32)
+
+
+def side_by_side(parts):
+    return parts.transpose(1, 0, 2).reshape(parts.shape[1], -1)
+
+
+def sum_all(array):
+    for swap in (swap_core, swap_chip):
+        array = array + swap(array)
+    for bit in range(lax.axis_size("band").bit_length() - 1):
+        array = array + swap_band(array, bit)
+    return array
 
 
 def slot_masks(counts, slot_waves, waves):
@@ -590,107 +951,40 @@
         partial_rows, kernel_table = embed_plain(
             counts, slot_waves, kernel_low, kernel_weight, pixels
         )
-    embedded_rows = (
-        rows_reduce(partial_rows)[:, :patches].reshape(-1, width) + conv_bias
-    )
-    row_count = embedded_rows.shape[0]
-    local_images = row_count // patches
-    head_size = width // HEADS
-    divisor = math.sqrt(head_size)
-    normed_in, norm_in_back = jax.vjp(block_norm, embedded_rows, attention_gain, attention_shift)
-    normed_low = normed_in.astype(jnp.bfloat16)
-    projected = jnp.dot(normed_low, block_qkv, preferred_element_type=jnp.float32).astype(
-        jnp.bfloat16
-    )
-    heads_view = projected.reshape(local_images, patches, 3, HEADS, head_size)
-    queries = heads_view[:, :, 0]
-    keys_all = heads_view[:, :, 1]
-    values_all = heads_view[:, :, 2]
-    scores = (
-        jnp.einsum("iqhd,ikhd->ihqk", queries, keys_all, preferred_element_type=jnp.float32)
-        / divisor
-    )
-    log_total = jax.nn.logsumexp(scores, axis=-1, keepdims=True)
-    probs_low = jnp.exp(scores - log_total).astype(jnp.bfloat16)
-    mixed_low = (
-        jnp.einsum("ihqk,ikhd->iqhd", probs_low, values_all, preferred_element_type=jnp.float32)
-        .reshape(row_count, width)
-        .astype(jnp.bfloat16)
-    )
-    middle = embedded_rows + jnp.dot(mixed_low, block_proj, preferred_element_type=jnp.float32)
-    normed_mid, norm_mid_back = jax.vjp(block_norm, middle, hidden_gain, hidden_shift)
-    mid_low = normed_mid.astype(jnp.bfloat16)
-    upward = jnp.dot(mid_low, block_up, preferred_element_type=jnp.float32)
-    activated, gelu_back = jax.vjp(exact_gelu, upward)
-    activated_low = activated.astype(jnp.bfloat16)
-    result = middle + jnp.dot(activated_low, block_down, preferred_element_type=jnp.float32)
-    layer_output = result.astype(jnp.bfloat16)
-    down_grad = jnp.einsum(
-        "rf,rd->fd", activated_low, cotangent, preferred_element_type=jnp.float32
-    )
-    grad_activated = jnp.einsum(
-        "rd,fd->rf", cotangent, block_down, preferred_element_type=jnp.float32
-    )
-    grad_up = gelu_back(grad_activated)[0].astype(jnp.bfloat16)
-    up_grad = jnp.einsum("rd,rf->df", mid_low, grad_up, preferred_element_type=jnp.float32)
-    grad_normed_mid = jnp.einsum("rf,df->rd", grad_up, block_up, preferred_element_type=jnp.float32)
-    grad_mid_norm, hidden_gain_part, hidden_shift_part = norm_mid_back(grad_normed_mid)
-    grad_middle = cotangent.astype(jnp.float32) + grad_mid_norm
-    grad_attended = grad_middle.astype(jnp.bfloat16)
-    proj_grad = jnp.einsum(
-        "re,rd->ed", mixed_low, grad_attended, preferred_element_type=jnp.float32
-    )
-    grad_mixed = jnp.einsum(
-        "rd,ed->re", grad_attended, block_proj, preferred_element_type=jnp.float32
-    ).astype(jnp.bfloat16)
-    grad_mixed_heads = grad_mixed.reshape(local_images, patches, HEADS, head_size)
-    again = (
-        jnp.einsum("iqhd,ikhd->ihqk", queries, keys_all, preferred_element_type=jnp.float32)
-        / divisor
-    )
-    probs_again = jnp.exp(again - log_total)
-    grad_probs = jnp.einsum(
-        "iqhd,ikhd->ihqk", grad_mixed_heads, values_all, preferred_element_type=jnp.float32
-    )
-    grad_values = jnp.einsum(
-        "ihqk,iqhd->ikhd",
-        probs_again.astype(jnp.bfloat16),
-        grad_mixed_heads,
-        preferred_element_type=jnp.float32,
-    )
-    grad_scores = (
-        probs_again * (grad_probs - jnp.sum(grad_probs * probs_again, axis=-1, keepdims=True))
-    ).astype(jnp.bfloat16)
-    grad_queries = (
-        jnp.einsum("ihqk,ikhd->iqhd", grad_scores, keys_all, preferred_element_type=jnp.float32)
-        / divisor
-    )
-    grad_keys = (
-        jnp.einsum("ihqk,iqhd->ikhd", grad_scores, queries, preferred_element_type=jnp.float32)
-        / divisor
-    )
-    grad_projected = (
-        jnp.stack([grad_queries, grad_keys, grad_values], axis=2)
-        .reshape(row_count, 3 * width)
-        .astype(jnp.bfloat16)
-    )
-    qkv_grad = jnp.einsum(
-        "rd,re->de", normed_low, grad_projected, preferred_element_type=jnp.float32
-    )
-    grad_normed_in = jnp.einsum(
-        "re,de->rd", grad_projected, block_qkv, preferred_element_type=jnp.float32
-    )
-    grad_in_norm, attention_gain_part, attention_shift_part = norm_in_back(grad_normed_in)
-    grad_embedded = grad_middle + grad_in_norm
-    grad_rows = jnp.pad(
-        grad_embedded.astype(jnp.bfloat16).reshape(local_images, patches, width),
-        ((0, 0), (0, pad_rows(patches) - patches), (0, 0)),
-    )
-    gathered = rows_gather(grad_rows)
-    block_down_grad = weight_reduce(down_grad)
-    block_up_grad = weight_reduce(up_grad)
-    block_proj_grad = weight_reduce(proj_grad)
-    block_qkv_grad = weight_reduce(qkv_grad)
+    padded = pad_rows(patches)
+    near, far = rows_reduce(partial_rows)
+    local_images = near.shape[0]
+    cot = jnp.pad(
+        cotangent.reshape(local_images, patches, width), ((0, 0), (0, padded - patches), (0, 0))
+    ).reshape(-1, width)
+    x, normed, projected, probs, mixed, middle, normed_mid = attend_call(
+        near.reshape(-1, width),
+        far.reshape(-1, width),
+        conv_bias,
+        attention_gain,
+        attention_shift,
+        block_qkv,
+        block_proj,
+        hidden_gain,
+        hidden_shift,
+        padded,
+        patches,
+    )
+    result, grad_middle, grad_low, down_part, up_part, hidden_gain_part, hidden_shift_part = (
+        mlp_call(normed_mid, middle, cot, hidden_gain, block_up, block_down)
+    )
+    layer_output = result.reshape(local_images, padded, width)[:, :patches].reshape(-1, width)
+    grad_x, grad_projected, bias_part, attention_gain_part, attention_shift_part = (
+        attend_back_call(
+            grad_low, grad_middle, x, projected, probs, attention_gain, block_qkv, block_proj, padded
+        )
+    )
+    attend_part = attend_weights_call(normed, mixed, grad_projected, grad_low)
+    gathered = rows_gather(grad_x.reshape(local_images, padded, width))
+    block_down_grad = weight_reduce(down_part[None], False)[0]
+    block_up_grad = side_by_side(weight_reduce(up_part, True))
+    attend_grads = weight_reduce(attend_part, True)
+    block_qkv_grad, block_proj_grad = side_by_side(attend_grads[:3]), attend_grads[3]
     if fits:
         pixel_grad, kernel_grad, in_part = embed_back_call(
             counts, slot_waves, gathered, kernel_table, wave_sums, pixels, kernel_weight
@@ -699,24 +993,24 @@
         pixel_grad, kernel_grad, in_part = embed_back_plain(
             counts, slot_waves, gathered, kernel_table, pixels, kernel_weight
         )
-    vectors = jnp.stack(
+    vectors = jnp.concatenate(
         [
-            jnp.sum(grad_embedded, axis=0),
+            bias_part,
             attention_gain_part,
             attention_shift_part,
             hidden_gain_part,
             hidden_shift_part,
         ]
     )
-    summed = lax.psum(
-        jnp.concatenate([in_part, vectors.reshape(-1, in_part.shape[1])], axis=0),
-        ("band", "rows"),
+    summed = sum_all(
+        jnp.concatenate([in_part, vectors.reshape(-1, in_part.shape[1])], axis=0)
     )
     grad_kernel_in = summed[:waves]
     bias_grad, attention_gain_grad, attention_shift_grad, hidden_gain_grad, hidden_shift_grad = (
         summed[waves:].reshape(5, width)
     )
-    owned = lax.psum_scatter(kernel_grad, "band", scatter_dimension=0, tiled=True)
+    bands = lax.axis_size("band")
+    owned = band_halve(kernel_grad.reshape(bands, -1, waves, width), 0)[0]
     owned_weight = jnp.einsum(
         "wk,qwc->qkc", kernel_low, owned, preferred_element_type=jnp.float32
     ).astype(jnp.bfloat16)

time: 678 us -> 480 us (0.71)
  Pallas kernels: 62.4 us -> 169 us
  matrix products: 126 us -> 20.4 us
  local copies, waits for them, and re-layouts: 136 us -> 61.8 us
  waiting for transfers between devices: 198 us -> 155 us
  blocking collectives: 42.1 us -> 0 us
  other arithmetic: 72 us -> 34 us
  starting transfers between devices: 18.7 us -> 32.9 us
  between operations: 15.4 us -> 2.11 us
    reduce_scatter x5 -> x0, waiting for transfers between devices: 147 us -> none  [the longest x4 147 us: weight_reduce(): part = lax.psum_scatter(pair, 'band', scatter_dimension=0, tiled=True)]
    pallas_call x0 -> x4, Pallas kernels: none -> 107 us  [the longest x1 35 us: mlp_call(): pl.pallas_call(mlp_kernel, grid=(steps,), in_specs=[whole(rows, width), w...]
    dot_general x18 -> x0, matrix products: 90.4 us -> none  [the longest x1 20.7 us: body(): jnp.einsum('rd,fd->rf', cotangent, block_down, preferred_element_type=jnp...]
    ppermute x0 -> x15, waiting for transfers between devices: none -> 86.7 us  [swap_band(): lax.ppermute(array, 'band', [(i, i ^ 1 << bit) for i in range(count)])]
    psum x1 -> x0, blocking collectives: 42.1 us -> none  [body(): lax.psum(jnp.concatenate([in_part, vectors.reshape(-1, in_part.shape[1])]...]
    unnamed x175 -> x131, local copies, waits for them, and re-layouts: 55.3 us -> 28.4 us
    convert_element_type x5 -> x0, local copies, waits for them, and re-layouts: 23.8 us -> none  [the longest x2 15.4 us: body(): grad_projected = jnp.stack([grad_queries, grad_keys, grad_values], axis=2...]
    convert_element_type x18 -> x17, other arithmetic: 42.9 us -> 20.1 us  [the longest x13 13.7 us: halve(): return add_wide(kept, swap(sent)).astype(array.dtype)]
  transfers between devices with their start and end apart: 24 -> 35, of which waited for: 8 -> 15; matrix products, arithmetic and copies ran while one was open for 21% -> 17% of each run, Pallas kernels for 5% -> 2%
where the time goes in v2:
time: 480 us; the launch traced here: 475 us
  Pallas kernels  169 us (35%)
  waiting for transfers between devices  155 us (32%)
  local copies, waits for them, and re-layouts  61.8 us (13%)
  other arithmetic  34 us (7%)
  starting transfers between devices  32.9 us (7%)
  matrix products  20.4 us (4%)
    ppermute x15, waiting for transfers between devices, swap_band(): lax.ppermute(array, 'band', [(i, i ^ 1 << bit) for i in range(count)])  86.7 us
    ppermute x8, waiting for transfers between devices, swap_chip(): return lax.ppermute(array, 'rows', [(0, 2), (2, 0), (1, 3), (3, 1)])  64.3 us
    pallas_call x1, Pallas kernels, mlp_call(): pl.pallas_call(mlp_kernel, grid=(steps,), in_specs=[whole(rows, width), w...  35 us
    pallas_call x1, Pallas kernels, embed_back_call(): pl.pallas_call(embed_back_kernel, grid=(2 * STEPS,), in_specs=[smem, smem...  33.5 us
    pallas_call x1, Pallas kernels, attend_call(): pl.pallas_call(functools.partial(attend_kernel, padded=padded, patches=pa...  32.7 us
    pallas_call x1, Pallas kernels, attend_back_call(): pl.pallas_call(functools.partial(attend_back_kernel, padded=padded), out_...  31.3 us
    pallas_call x1, Pallas kernels, embed_call(): pl.pallas_call(embed_kernel, grid=(STEPS,), in_specs=[smem, smem, pl.Bloc...  28.6 us
    unnamed x131, local copies, waits for them, and re-layouts  28.4 us
  transfers between devices with their start and end apart: 35, of which 15 were waited for; matrix products, arithmetic and copies ran while one was open for 17% of the time, Pallas kernels for 2%

profile of v2, /device:TPU:0, one launch (start us, length us, event | category | flops | bytes accessed | tf_op | source)
XLA Modules:
  0.0 475.4 jit_solution(16255030691791579524)
XLA Ops:
  9.3 13.5 %copy.111.pix_ref = bf16[256,64,196]{2,1,0:T(8,128)(2,1)} copy(bf16[256,64,196]{0,1,2:T(8,128)(2,1)} %param.24) | data formatting | bytes 12845056 | tf_op args[0]
  22.8 28.6 %embed.1 = (bf16[12,208,768]{2,1,0:T(8,128)(2,1)}, bf16[32,64,196]{2,1,0:T(8,128)(2,1)}, bf16[32,64,768]{2,1,0:T(8,128)(2,1)}) custom-call(s32[12]{0:T(128)} %bitcast.180, s32[256]{0:T(256)} %bitcast.178, bf16[32,128]{1,0:T(8,128)(2,1)} %fusion.28.kin_ref, bf16[64,128,768]{2,1,0:T(8,128)(2,1)} %weight_ref.3, bf16[256,64,196]{2,1,0:T(8,128)(2,1)} %copy.111.pix_ref), custom_call_target="tpu_custom_call" | custom-call | tf_op jit(solution)/shard_map/embed/pallas_call | solution.py:142
  51.4 2.9 constant_dynamic-slice_fusion.18
  54.8 2.4 collective-permute-done
  58.6 4.0 add_convert_fusion.7
  62.6 2.9 collective-permute-start.2
  71.7 15.6 %collective-permute-done.2 = bf16[3,208,768]{2,1,0:T(8,128)(2,1)} collective-permute-done((bf16[3,208,768]{2,1,0:T(8,128)(2,1)}, bf16[3,208,768]{2,1,0:T(8,128)(2,1)}, u32[]{:S(2)}, u32[]{:S(2)}) %collective-permute-start.2) | collective-permute-done | bytes 958496 | tf_op jit(solution)/shard_map/ppermute | solution.py:724
  87.3 32.7 %attend.1 = (f32[624,768]{1,0:T(8,128)}, bf16[624,768]{1,0:T(8,128)(2,1)}, bf16[624,2304]{1,0:T(8,128)(2,1)}, bf16[36,208,208]{2,1,0:T(8,128)(2,1)}, bf16[624,76...) custom-call(f32[624,768]{1,0:T(8,128)} %bitcast.135, bf16[624,768]{1,0:T(8,128)(2,1)} %bitcast.9.far_ref, ...), custom_call_target="tpu_custom_call" | custom-call | tf_op jit(solution)/shard_map/attend/pallas_call | solution.py:452
  120.0 35.0 %mlp.1 = (bf16[624,768]{1,0:T(8,128)(2,1)}, f32[624,768]{1,0:T(8,128)}, bf16[624,768]{1,0:T(8,128)(2,1)}, bf16[3072,768]{1,0:T(8,128)(2,1)}, bf16[4,768,768]{2,1...) custom-call(bf16[624,768]{1,0:T(8,128)(2,1)} %get-tuple-element.47.normed_ref, ...), custom_call_target="tpu_custom_call" | custom-call | tf_op jit(solution)/shard_map/mlp/pallas_call | solution.py:514
  155.0 31.3 %attend_back.1 = (bf16[624,768]{1,0:T(8,128)(2,1)}, bf16[624,2304]{1,0:T(8,128)(2,1)}, f32[1,768]{1,0:T(1,128)}, f32[1,768]{1,0:T(1,128)}, f32[1,768]{1,0:T(1,128)}) custom-call(bf16[624,768]{1,0:T(8,128)(2,1)} %get-tuple-element.50.low_ref, f32[624,768]{1,0:T(8,128)} %get-tuple-element.51.grad_ref, f32[624,768]{1,0:T(8,128)} %get-tuple-element.52.x_ref, ...), custom_call_target="tpu_custom_call" | custom-call | tf_op jit(solution)/shard_map/attend_back/pallas_call | solution.py:620
  188.0 21.3 %collective-permute-done.4 = bf16[3,208,768]{2,1,0:T(8,128)(2,1)} collective-permute-done((bf16[3,208,768]{2,1,0:T(8,128)(2,1)}, bf16[3,208,768]{2,1,0:T(8,128)(2,1)}, u32[]{:S(2)}, u32[]{:S(2)}) %collective-permute-start.4) | collective-permute-done | bytes 958496 | tf_op jit(solution)/shard_map/ppermute | solution.py:724
  215.0 2.2 pad_maximum_fusion.grad_ref
  217.2 33.5 %embed_back.1 = (bf16[256,64,196]{2,1,0:T(8,128)(2,1)}, bf16[64,32,768]{2,1,0:T(8,128)(2,1)}, f32[32,128]{1,0:T(8,128)}) custom-call(s32[12]{0:T(128)} %bitcast.181, s32[256]{0:T(256)} %bitcast.179, bf16[12,208,768]{2,1,0:T(8,128)(2,1)} %pad_maximum_fusion.grad_ref, bf16[32,64,768]{2,1,0:T(8,128)(2,1)} %get-tuple-element.56.table_ref, ...), custom_call_target="tpu_custom_call" | custom-call | tf_op jit(solution)/shard_map/embed_back/pallas_call | solution.py:305
  254.2 3.3 constant_dynamic-slice_fusion.2
  257.6 8.2 %attend_weights.1 = bf16[4,768,768]{2,1,0:T(8,128)(2,1)} custom-call(bf16[624,768]{1,0:T(8,128)(2,1)} %get-tuple-element.66.normed_ref, bf16[624,768]{1,0:T(8,128)(2,1)} %get-tuple-element.67.mixed_ref, bf16[624,2304]{1,0:T(8,128)(2,1)} %get-tuple-element.68.grad_projected_ref, bf16[624,768]{1,0:T(8,128)(2,1)} %get-tuple-element.50.low_ref), custom_call_target="tpu_custom_call" | custom-call | tf_op jit(solution)/shard_map/attend_weights/pallas_call | solution.py:643
  267.1 3.4 constant_dynamic-slice_fusion.14
  272.7 3.4 constant_dynamic-slice_fusion.8
  278.0 3.1 collective-permute-start.13
  281.1 2.7 constant_dynamic-slice_fusion.17
  284.7 13.6 %copy.129 = bf16[256,64,196]{0,1,2:T(8,128)(2,1)} copy(bf16[256,64,196]{2,1,0:T(8,128)(2,1)} %get-tuple-element.135) | data formatting | bytes 12845056
  308.8 2.8 fusion.15
  311.6 3.0 add_convert_fusion
  316.0 2.4 add_convert_fusion.2
  319.1 2.5 add_convert_fusion.1
  327.6 18.1 %collective-permute-done.29 = bf16[1,4,1,384,384]{4,3,1,2,0:T(8,128)(2,1)S(1)} collective-permute-done((bf16[1,4,1,384,384]{4,3,1,2,0:T(8,128)(2,1)S(1)}, bf16[1,4,1,384,384]{4,3,1,2,0:T(8,128)(2,1)S(1)}, u32[]{:S(2)}, u32[]{:S(2)}) %collective-permute-start.29) | collective-permute-done | bytes 1179680 | tf_op jit(solution)/shard_map/ppermute | solution.py:766
  347.7 24.0 %collective-permute-done.22 = bf16[4,8,48,384]{3,2,1,0:T(8,128)(2,1)S(1)} collective-permute-done((bf16[4,8,48,384]{3,2,1,0:T(8,128)(2,1)S(1)}, bf16[4,8,48,384]{3,2,1,0:T(8,128)(2,1)S(1)}, u32[]{:S(2)}, u32[]{:S(2)}) %collective-permute-start.22) | collective-permute-done | bytes 1179680 | tf_op jit(solution)/shard_map/ppermute | solution.py:724
  376.2 12.5 %collective-permute-done.23 = bf16[4,4,1,48,384]{4,3,0,1,2:T(8,128)(2,1)S(1)} collective-permute-done((bf16[4,4,1,48,384]{4,3,0,1,2:T(8,128)(2,1)S(1)}, bf16[4,4,1,48,384]{4,3,0,1,2:T(8,128)(2,1)S(1)}, u32[]{:S(2)}, u32[]{:S(2)}) %collective-permute-start.23) | collective-permute-done | bytes 589856 | tf_op jit(solution)/shard_map/ppermute | solution.py:766
  391.0 8.4 %collective-permute-done.16 = bf16[4,4,1,48,384]{4,3,0,1,2:T(8,128)(2,1)S(1)} collective-permute-done((bf16[4,4,1,48,384]{4,3,0,1,2:T(8,128)(2,1)S(1)}, bf16[4,4,1,48,384]{4,3,0,1,2:T(8,128)(2,1)S(1)}, u32[]{:S(2)}, u32[]{:S(2)}) %collective-permute-start.16) | collective-permute-done | bytes 589856 | tf_op jit(solution)/shard_map/ppermute | solution.py:766
  401.5 5.9 %collective-permute-done.8 = bf16[1,1,8,32,768]{4,3,2,1,0:T(8,128)(2,1)S(1)} collective-permute-done((bf16[1,1,8,32,768]{4,3,2,1,0:T(8,128)(2,1)S(1)}, bf16[1,1,8,32,768]{4,3,2,1,0:T(8,128)(2,1)S(1)}, u32[]{:S(2)}, u32[]{:S(2)}) %collective-permute-start.8) | collective-permute-done | bytes 393248 | tf_op jit(solution)/shard_map/ppermute | solution.py:766
  409.9 3.6 all-to-all-start
  414.6 2.9 collective-permute-start.25
  418.8 40.9 %collective-permute-done.25 = bf16[4,1,1,48,384]{4,3,0,2,1:T(8,128)(2,1)S(1)} collective-permute-done((bf16[4,1,1,48,384]{4,3,0,2,1:T(8,128)(2,1)S(1)}, bf16[4,1,1,48,384]{4,3,0,2,1:T(8,128)(2,1)S(1)}, u32[]{:S(2)}, u32[]{:S(2)}) %collective-permute-start.25) | collective-permute-done | bytes 147488 | tf_op jit(solution)/shard_map/ppermute | solution.py:766
  (294 shorter events, 83.1 us)
Async XLA Ops:
  54.7 3.9 collective-permute-start.1
  62.6 24.7 %collective-permute-start.2 = (bf16[3,208,768]{2,1,0:T(8,128)(2,1)}, bf16[3,208,768]{2,1,0:T(8,128)(2,1)}, u32[]{:S(2)}, u32[]{:S(2)}) collective-permute-start(bf16[3,208,768]{2,1,0:T(8,128)(2,1)} %get-tuple-element.167), channel_id=1, source_target_pairs={{0,2},{2,0},{1,3},{3,1},{4,6},{6,4},{5,7},{7,5},{8,10},{10,8},{9,1... | collective-permute-start | bytes 2875400 | tf_op jit(solution)/shard_map/ppermute | solution.py:724
  186.3 23.1 %collective-permute-start.4 = (bf16[3,208,768]{2,1,0:T(8,128)(2,1)}, bf16[3,208,768]{2,1,0:T(8,128)(2,1)}, u32[]{:S(2)}, u32[]{:S(2)}) collective-permute-start(bf16[3,208,768]{2,1,0:T(8,128)(2,1)} %bitcast.161), channel_id=1, source_target_pairs={{0,2},{2,0},{1,3},{3,1},{4,6},{6,4},{5,7},{7,5},{8,10},{10,8},{9,1... | collective-permute-start | bytes 2875400 | tf_op jit(solution)/shard_map/ppermute | solution.py:724
  188.0 23.3 %collective-permute-start.3 = (bf16[3,208,768]{2,1,0:T(8,128)(2,1)}, bf16[3,208,768]{2,1,0:T(8,128)(2,1)}, u32[]{:S(2)}, u32[]{:S(2)}) collective-permute-start(bf16[3,208,768]{2,1,0:T(8,128)(2,1)} %bitcast.162), channel_id=1, source_target_pairs={{0,1},{1,0},{2,3},{3,2},{4,5},{5,4},{6,7},{7,6},{8,9},{9,8},{10,11... | collective-permute-start | bytes 2875400 | tf_op jit(solution)/shard_map/ppermute | solution.py:720
  209.4 3.6 collective-permute-start.5
  252.8 13.0 %collective-permute-start.10 = (f32[62,128]{1,0:T(8,128)S(1)}, f32[62,128]{1,0:T(8,128)S(1)}, u32[]{:S(2)}, u32[]{:S(2)}) collective-permute-start(f32[62,128]{1,0:T(8,128)S(1)} %add.249), channel_id=1, source_target_pairs={{0,2},{2,0},{1,3},{3,1},{4,6},{6,4},{5,7},{7,5},{8,10},{10,8},{9,1... | collective-permute-start | bytes 95240 | tf_op jit(solution)/shard_map/ppermute | solution.py:724
  257.5 54.1 %collective-permute-start.28 = (bf16[1,8,384,384]{3,2,1,0:T(8,128)(2,1)}, bf16[1,8,384,384]{3,2,1,0:T(8,128)(2,1)}, u32[]{:S(2)}, u32[]{:S(2)}) collective-permute-start(bf16[1,8,384,384]{3,2,1,0:T(8,128)(2,1)} %constant_dynamic-slice_fusion.2), channel_id=1, source_target_pairs={{0,1},{1,0},{2,3},{3,2},{4,5},{5,4},{6,7},{7,6},{8,9},{9,8},{10,11... | collective-permute-start | bytes 7077896 | tf_op jit(solution)/shard_map/ppermute | solution.py:720
  265.8 4.9 %collective-permute-start.11 = (f32[62,128]{1,0:T(8,128)S(1)}, f32[62,128]{1,0:T(8,128)S(1)}, u32[]{:S(2)}, u32[]{:S(2)}) collective-permute-start(f32[62,128]{1,0:T(8,128)S(1)} %add.250), channel_id=1, source_target_pairs={{0,4},{4,0},{8,12},{12,8},{16,20},{20,16},{24,28},{28,24},{1,5},{5... | collective-permute-start | bytes 95240 | tf_op jit(solution)/shard_map/ppermute | solution.py:766
  270.5 45.5 %collective-permute-start.14 = (bf16[4,8,96,384]{3,2,1,0:T(8,128)(2,1)}, bf16[4,8,96,384]{3,2,1,0:T(8,128)(2,1)}, u32[]{:S(2)}, u32[]{:S(2)}) collective-permute-start(bf16[4,8,96,384]{3,2,1,0:T(8,128)(2,1)} %constant_dynamic-slice_fusion.14), channel_id=1, source_target_pairs={{0,1},{1,0},{2,3},{3,2},{4,5},{5,4},{6,7},{7,6},{8,9},{9,8},{10,11... | collective-permute-start | bytes 7077896 | tf_op jit(solution)/shard_map/ppermute | solution.py:720
  271.3 5.9 %collective-permute-start.12 = (f32[62,128]{1,0:T(8,128)}, f32[62,128]{1,0:T(8,128)}, u32[]{:S(2)}, u32[]{:S(2)}) collective-permute-start(f32[62,128]{1,0:T(8,128)} %add.251), channel_id=1, source_target_pairs={{0,8},{4,12},{8,0},{12,4},{16,24},{20,28},{24,16},{28,20},{1,9},{5... | collective-permute-start | bytes 95240 | tf_op jit(solution)/shard_map/ppermute | solution.py:766
  276.1 43.0 %collective-permute-start.21 = (bf16[4,8,96,384]{3,2,1,0:T(8,128)(2,1)}, bf16[4,8,96,384]{3,2,1,0:T(8,128)(2,1)}, u32[]{:S(2)}, u32[]{:S(2)}) collective-permute-start(bf16[4,8,96,384]{3,2,1,0:T(8,128)(2,1)} %constant_dynamic-slice_fusion.8), channel_id=1, source_target_pairs={{0,1},{1,0},{2,3},{3,2},{4,5},{5,4},{6,7},{7,6},{8,9},{9,8},{10,11... | collective-permute-start | bytes 7077896 | tf_op jit(solution)/shard_map/ppermute | solution.py:720
  278.0 20.3 %collective-permute-start.13 = (f32[62,128]{1,0:T(8,128)S(1)}, f32[62,128]{1,0:T(8,128)S(1)}, u32[]{:S(2)}, u32[]{:S(2)}) collective-permute-start(f32[62,128]{1,0:T(8,128)S(1)} %add.252), channel_id=1, source_target_pairs={{0,16},{4,20},{8,24},{12,28},{16,0},{20,4},{24,8},{28,12},{1,17},{... | collective-permute-start | bytes 95240 | tf_op jit(solution)/shard_map/ppermute | solution.py:766
  283.7 40.8 %collective-permute-start.6 = (bf16[4,1,8,32,768]{4,3,2,1,0:T(8,128)(2,1)}, bf16[4,1,8,32,768]{4,3,2,1,0:T(8,128)(2,1)}, u32[]{:S(2)}, u32[]{:S(2)}) collective-permute-start(bf16[4,1,8,32,768]{4,3,2,1,0:T(8,128)(2,1)} %constant_dynamic-slice_fusion.17), channel_id=1, source_target_pairs={{0,4},{4,0},{8,12},{12,8},{16,20},{20,16},{24,28},{28,24},{1,5},{5... | collective-permute-start | bytes 4718600 | tf_op jit(solution)/shard_map/ppermute | solution.py:766
  314.8 30.9 %collective-permute-start.29 = (bf16[1,4,1,384,384]{4,3,1,2,0:T(8,128)(2,1)S(1)}, bf16[1,4,1,384,384]{4,3,1,2,0:T(8,128)(2,1)S(1)}, u32[]{:S(2)}, u32[]{:S(2)}) collective-permute-start(bf16[1,4,1,384,384]{4,3,1,2,0:T(8,128)(2,1)S(1)} %dynamic-slice_bitcast_fusion), channel_id=1, source_target_pairs={{0,4},{4,0},{8,12},{12,8},{16,20},{20,16},{24,28},{28,24},{1,5},{5... | collective-permute-start | bytes 3538952 | tf_op jit(solution)/shard_map/ppermute | solution.py:766
  318.5 28.9 %collective-permute-start.15 = (bf16[4,8,48,384]{3,2,1,0:T(8,128)(2,1)S(1)}, bf16[4,8,48,384]{3,2,1,0:T(8,128)(2,1)S(1)}, u32[]{:S(2)}, u32[]{:S(2)}) collective-permute-start(bf16[4,8,48,384]{3,2,1,0:T(8,128)(2,1)S(1)} %constant_dynamic-slice_fusion.13), channel_id=1, source_target_pairs={{0,2},{2,0},{1,3},{3,1},{4,6},{6,4},{5,7},{7,5},{8,10},{10,8},{9,1... | collective-permute-start | bytes 3538952 | tf_op jit(solution)/shard_map/ppermute | solution.py:724
  321.8 49.9 %collective-permute-start.22 = (bf16[4,8,48,384]{3,2,1,0:T(8,128)(2,1)S(1)}, bf16[4,8,48,384]{3,2,1,0:T(8,128)(2,1)S(1)}, u32[]{:S(2)}, u32[]{:S(2)}) collective-permute-start(bf16[4,8,48,384]{3,2,1,0:T(8,128)(2,1)S(1)} %constant_dynamic-slice_fusion.7), channel_id=1, source_target_pairs={{0,2},{2,0},{1,3},{3,1},{4,6},{6,4},{5,7},{7,5},{8,10},{10,8},{9,1... | collective-permute-start | bytes 3538952 | tf_op jit(solution)/shard_map/ppermute | solution.py:724
  326.5 63.8 %collective-permute-start.7 = (bf16[2,1,8,32,768]{4,3,2,1,0:T(8,128)(2,1)S(1)}, bf16[2,1,8,32,768]{4,3,2,1,0:T(8,128)(2,1)S(1)}, u32[]{:S(2)}, u32[]{:S(2)}) collective-permute-start(bf16[2,1,8,32,768]{4,3,2,1,0:T(8,128)(2,1)S(1)} %constant_dynamic-slice_fusion.16), channel_id=1, source_target_pairs={{0,8},{4,12},{8,0},{12,4},{16,24},{20,28},{24,16},{28,20},{1,9},{5... | collective-permute-start | bytes 2359304 | tf_op jit(solution)/shard_map/ppermute | solution.py:766
  346.1 29.3 %collective-permute-start.30 = (bf16[1,2,1,384,384]{4,3,2,1,0:T(8,128)(2,1)S(1)}, bf16[1,2,1,384,384]{4,3,2,1,0:T(8,128)(2,1)S(1)}, u32[]{:S(2)}, u32[]{:S(2)}) collective-permute-start(bf16[1,2,1,384,384]{4,3,2,1,0:T(8,128)(2,1)S(1)} %constant_dynamic-slice_fusion.1), channel_id=1, source_target_pairs={{0,8},{4,12},{8,0},{12,4},{16,24},{20,28},{24,16},{28,20},{1,9},{5... | collective-permute-start | bytes 1769480 | tf_op jit(solution)/shard_map/ppermute | solution.py:766
  372.4 16.3 %collective-permute-start.23 = (bf16[4,4,1,48,384]{4,3,0,1,2:T(8,128)(2,1)S(1)}, bf16[4,4,1,48,384]{4,3,0,1,2:T(8,128)(2,1)S(1)}, u32[]{:S(2)}, u32[]{:S(2)}) collective-permute-start(bf16[4,4,1,48,384]{4,3,0,1,2:T(8,128)(2,1)S(1)} %copy.138), channel_id=1, source_target_pairs={{0,4},{4,0},{8,12},{12,8},{16,20},{20,16},{24,28},{28,24},{1,5},{5... | collective-permute-start | bytes 1769480 | tf_op jit(solution)/shard_map/ppermute | solution.py:766
  374.3 25.1 %collective-permute-start.16 = (bf16[4,4,1,48,384]{4,3,0,1,2:T(8,128)(2,1)S(1)}, bf16[4,4,1,48,384]{4,3,0,1,2:T(8,128)(2,1)S(1)}, u32[]{:S(2)}, u32[]{:S(2)}) collective-permute-start(bf16[4,4,1,48,384]{4,3,0,1,2:T(8,128)(2,1)S(1)} %copy.136), channel_id=1, source_target_pairs={{0,4},{4,0},{8,12},{12,8},{16,20},{20,16},{24,28},{28,24},{1,5},{5... | collective-permute-start | bytes 1769480 | tf_op jit(solution)/shard_map/ppermute | solution.py:766
  375.8 25.0 %collective-permute-start.31 = (bf16[1,1,1,384,384]{4,3,2,1,0:T(8,128)(2,1)S(1)}, bf16[1,1,1,384,384]{4,3,2,1,0:T(8,128)(2,1)S(1)}, u32[]{:S(2)}, u32[]{:S(2)}) collective-permute-start(bf16[1,1,1,384,384]{4,3,2,1,0:T(8,128)(2,1)S(1)} %constant_dynamic-slice_fusion), channel_id=1, source_target_pairs={{0,16},{4,20},{8,24},{12,28},{16,0},{20,4},{24,8},{28,12},{1,17},{... | collective-permute-start | bytes 884744 | tf_op jit(solution)/shard_map/ppermute | solution.py:766
  389.6 23.9 %collective-permute-start.24 = (bf16[4,2,1,48,384]{4,3,0,2,1:T(8,128)(2,1)}, bf16[4,2,1,48,384]{4,3,0,2,1:T(8,128)(2,1)}, u32[]{:S(2)}, u32[]{:S(2)}) collective-permute-start(bf16[4,2,1,48,384]{4,3,0,2,1:T(8,128)(2,1)} %constant_dynamic-slice_fusion.4), channel_id=1, source_target_pairs={{0,8},{4,12},{8,0},{12,4},{16,24},{20,28},{24,16},{28,20},{1,9},{5... | collective-permute-start | bytes 884744 | tf_op jit(solution)/shard_map/ppermute | solution.py:766
  390.6 16.7 %collective-permute-start.8 = (bf16[1,1,8,32,768]{4,3,2,1,0:T(8,128)(2,1)S(1)}, bf16[1,1,8,32,768]{4,3,2,1,0:T(8,128)(2,1)S(1)}, u32[]{:S(2)}, u32[]{:S(2)}) collective-permute-start(bf16[1,1,8,32,768]{4,3,2,1,0:T(8,128)(2,1)S(1)} %constant_dynamic-slice_fusion.15), channel_id=1, source_target_pairs={{0,16},{4,20},{8,24},{12,28},{16,0},{20,4},{24,8},{28,12},{1,17},{... | collective-permute-start | bytes 1179656 | tf_op jit(solution)/shard_map/ppermute | solution.py:766
  400.4 17.1 %collective-permute-start.17 = (bf16[4,2,1,48,384]{4,3,0,2,1:T(8,128)(2,1)}, bf16[4,2,1,48,384]{4,3,0,2,1:T(8,128)(2,1)}, u32[]{:S(2)}, u32[]{:S(2)}) collective-permute-start(bf16[4,2,1,48,384]{4,3,0,2,1:T(8,128)(2,1)} %constant_dynamic-slice_fusion.10), channel_id=1, source_target_pairs={{0,8},{4,12},{8,0},{12,4},{16,24},{20,28},{24,16},{28,20},{1,9},{5... | collective-permute-start | bytes 884744 | tf_op jit(solution)/shard_map/ppermute | solution.py:766
  400.9 65.8 %collective-permute-start.32 = (bf16[1,384,384]{2,1,0:T(8,128)(2,1)S(1)}, bf16[1,384,384]{2,1,0:T(8,128)(2,1)}, u32[]{:S(2)}, u32[]{:S(2)}) collective-permute-start(bf16[1,384,384]{2,1,0:T(8,128)(2,1)S(1)} %fusion.12), channel_id=1, source_target_pairs={{0,2},{2,0},{1,3},{3,1},{4,6},{6,4},{5,7},{7,5},{8,10},{10,8},{9,1... | collective-permute-start | bytes 884744 | tf_op jit(solution)/shard_map/ppermute | solution.py:724
  409.9 62.7 %all-to-all-start = ((bf16[8,128,768]{2,0,1:T(8,128)(2,1)}), bf16[8,128,768]{2,0,1:T(8,128)(2,1)S(1)}, u32[]{:S(2)}, u32[]{:S(2)}) async-start(bf16[8,128,768]{2,0,1:T(8,128)(2,1)} %copy.113), calls=%async_computation | async-start | bytes 3145728 | tf_op jit(solution)/shard_map/all_to_all | solution.py:1017
  414.6 45.1 %collective-permute-start.25 = (bf16[4,1,1,48,384]{4,3,0,2,1:T(8,128)(2,1)S(1)}, bf16[4,1,1,48,384]{4,3,0,2,1:T(8,128)(2,1)S(1)}, u32[]{:S(2)}, u32[]{:S(2)}) collective-permute-start(bf16[4,1,1,48,384]{4,3,0,2,1:T(8,128)(2,1)S(1)} %constant_dynamic-slice_fusion.3), channel_id=1, source_target_pairs={{0,16},{4,20},{8,24},{12,28},{16,0},{20,4},{24,8},{28,12},{1,17},{... | collective-permute-start | bytes 442376 | tf_op jit(solution)/shard_map/ppermute | solution.py:766
  418.7 42.6 %collective-permute-start.18 = (bf16[4,1,1,48,384]{4,3,0,2,1:T(8,128)(2,1)S(1)}, bf16[4,1,1,48,384]{4,3,0,2,1:T(8,128)(2,1)S(1)}, u32[]{:S(2)}, u32[]{:S(2)}) collective-permute-start(bf16[4,1,1,48,384]{4,3,0,2,1:T(8,128)(2,1)S(1)} %constant_dynamic-slice_fusion.9), channel_id=1, source_target_pairs={{0,16},{4,20},{8,24},{12,28},{16,0},{20,4},{24,8},{28,12},{1,17},{... | collective-permute-start | bytes 442376 | tf_op jit(solution)/shard_map/ppermute | solution.py:766
  459.7 5.2 %collective-permute-start.26 = (bf16[4,48,384]{2,1,0:T(8,128)(2,1)S(1)}, bf16[4,48,384]{2,1,0:T(8,128)(2,1)S(1)}, u32[]{:S(2)}, u32[]{:S(2)}) collective-permute-start(bf16[4,48,384]{2,1,0:T(8,128)(2,1)S(1)} %fusion.14), channel_id=1, source_target_pairs={{0,2},{2,0},{1,3},{3,1},{4,6},{6,4},{5,7},{7,5},{8,10},{10,8},{9,1... | collective-permute-start | bytes 442376 | tf_op jit(solution)/shard_map/ppermute | solution.py:724
  461.3 5.2 %collective-permute-start.19 = (bf16[4,48,384]{2,1,0:T(8,128)(2,1)S(1)}, bf16[4,48,384]{2,1,0:T(8,128)(2,1)S(1)}, u32[]{:S(2)}, u32[]{:S(2)}) collective-permute-start(bf16[4,48,384]{2,1,0:T(8,128)(2,1)S(1)} %fusion.13), channel_id=1, source_target_pairs={{0,2},{2,0},{1,3},{3,1},{4,6},{6,4},{5,7},{7,5},{8,10},{10,8},{9,1... | collective-permute-start | bytes 442376 | tf_op jit(solution)/shard_map/ppermute | solution.py:724
  465.0 3.3 collective-permute-start.27
  467.7 3.0 collective-permute-start.33
  (65 other events, 627.1 us)
